TPU v7x, 512 devices: a whole 4x4x16 slice. The times are simulated.
512 devices in a mesh: gx: 16 (over z_hi, x, core), gy: 32 (over y, z_lo).
Axes of the slice: x: 4, y: 4, z: 16 (z_hi: 2, z_lo: 8; z = z_hi * 8 + z_lo), core: 2. Of those that a mesh axis runs over, the one named last changes fastest.
Arguments:
- flow: float32 [5, 1024, 4096], P(None, 'gx', 'gy'), as said below
- vib: float32 [46, 1024, 4096], P(None, 'gx', 'gy'), may hold values from 0.2 to 2
- species: float32 [30, 1024, 4096], P(None, 'gx', 'gy'), may hold values from 0.2 to 2
- field_rate: float32 [1024, 4096], P('gx', 'gy'), may hold values from 0.25 to 2
- substeps: int32 [1024, 32], P('gx', 'gy'), may hold values from 2 to 16, as said below
- vib_rates: float32 [46, 46], replicated, as said below
- kin_rates: float32 [30, 30], replicated, as said below
- level_energy: float32 [46], replicated, may hold values from 0 to 0.05
- formation_heat: float32 [30], replicated, may hold values from 0 to 0.05
Outputs:
- new_flow: float32 [5, 1024, 4096], P(None, 'gx', 'gy')
- vib_final: float32 [46, 1024, 4096], P(None, 'gx', 'gy')
- species_final: float32 [30, 1024, 4096], P(None, 'gx', 'gy')
Inputs may be any that keep to these rules, and one draw needn't show every extreme that they name: Blocks in the tile columns within 4 columns (periodic) of one column drawn from the seed take exactly 16 substeps; all others take 2 to 5. `flow`: density and pressure are at least 0.5 in every cell. `vib_rates`: diagonal entries between -2.5 and -1.5, off-diagonal ones between 0 and 1 / 46. `kin_rates`: diagonal entries between -2.5 and -1.5, off-diagonal ones between 0 and 1 / 30.
All inputs are finite; a program needn't handle non-finite values.
Results may differ from a plain program's by a relative error of at most 0.0001.
Values sent between devices are 32-bit elements; how exact they have to be, the bound alone decides.
No kernel may reach another device: no remote copies, remote signals or barrier semaphores. Data moves between devices by JAX's collectives and lax.ppermute only.
A program may use at most 64 MiB of HBM per device.

v0:
```python
import jax
import jax.numpy as jnp
from jax import lax
from jax.sharding import PartitionSpec as P

GAMMA = 1.4
COURANT = 0.1
H_CHEM = 0.05
EPS_W = 1e-06
HIGH = lax.Precision.HIGHEST


def from_partner(value, axis, stride):
    mask = 2**stride
    pairs = [(source, source ^ mask) for source in range(lax.axis_size(axis))]
    return lax.ppermute(value, axis, pairs)


def padded_2(value, sides, width):
    for axis, dim in sides:
        size, length = (lax.axis_size(axis), value.shape[dim])
        up = [(i, (i + 1) % size) for i in range(size)]
        down = [(j, i) for i, j in up]
        last = lax.slice_in_dim(value, length - width, length, axis=dim)
        leading = lax.slice_in_dim(value, 0, width, axis=dim)
        before = lax.ppermute(last, axis, up)
        after = lax.ppermute(leading, axis, down)
        value = jnp.concatenate([before, value, after], axis=dim)
    return value


def fluxes(q):
    rho = q[0]
    speed_u = q[1] / rho
    kinetic = 0.5 * (q[1] * q[1] + q[2] * q[2] + q[3] * q[3]) / rho
    press = (GAMMA - 1.0) * (q[4] - kinetic)
    flux = jnp.stack(
        [q[1], q[1] * speed_u + press, q[2] * speed_u, q[3] * speed_u, (q[4] + press) * speed_u]
    )
    speed = jnp.abs(speed_u) + jnp.sqrt(GAMMA * press / rho)
    return (flux, speed)


def weno_face(v0, v1, v2, v3, v4):
    p0 = (2.0 * v0 - 7.0 * v1 + 11.0 * v2) / 6.0
    p1 = (-v1 + 5.0 * v2 + 2.0 * v3) / 6.0
    p2 = (2.0 * v2 + 5.0 * v3 - v4) / 6.0
    b0 = 13.0 / 12.0 * (v0 - 2.0 * v1 + v2) ** 2 + 0.25 * (v0 - 4.0 * v1 + 3.0 * v2) ** 2
    b1 = 13.0 / 12.0 * (v1 - 2.0 * v2 + v3) ** 2 + 0.25 * (v1 - v3) ** 2
    b2 = 13.0 / 12.0 * (v2 - 2.0 * v3 + v4) ** 2 + 0.25 * (3.0 * v2 - 4.0 * v3 + v4) ** 2
    a0 = 0.1 / (EPS_W + b0) ** 2
    a1 = 0.6 / (EPS_W + b1) ** 2
    a2 = 0.3 / (EPS_W + b2) ** 2
    return (a0 * p0 + a1 * p1 + a2 * p2) / (a0 + a1 + a2)


def divergence(q):
    count = q.shape[1] - 6
    flux, speed = fluxes(q)
    speed3 = speed[None]

    def take(arr, offset):
        return arr[:, offset : offset + count + 1]

    alpha = take(speed3, 0)
    for offset in range(1, 6):
        alpha = jnp.maximum(alpha, take(speed3, offset))
    plus = [0.5 * (take(flux, o) + alpha * take(q, o)) for o in range(0, 5)]
    minus = [0.5 * (take(flux, o) - alpha * take(q, o)) for o in range(1, 6)]
    face = weno_face(*plus) + weno_face(minus[4], minus[3], minus[2], minus[1], minus[0])
    return face[:, 1:] - face[:, :-1]


def permute(q):
    return jnp.stack([q[0], q[2], q[1], q[3], q[4]])


def advance(padded):
    along_x = divergence(padded[:, :, 3:-3])
    turned = permute(jnp.swapaxes(padded[:, 3:-3, :], 1, 2))
    along_y = jnp.swapaxes(permute(divergence(turned)), 1, 2)
    return padded[:, 3:-3, 3:-3] - COURANT * (along_x + along_y)


def react(levels, dens, rate_rows, counts, vib_rates, kin_rates):
    rows = rate_rows.shape[0]
    width = rate_rows.shape[1]
    num_levels = levels.shape[0]
    num_species = dens.shape[0]
    flat_v = levels.reshape(num_levels, rows * width)
    flat_s = dens.reshape(num_species, rows * width)
    rates = rate_rows.reshape(rows * width)
    cell_counts = jnp.repeat(counts, width)
    trips = jnp.max(counts)

    def substep(k, state):
        cur_v, cur_s = state
        live = k < cell_counts
        prod_v = jnp.dot(vib_rates, cur_v, precision=HIGH)
        prod_s = jnp.dot(kin_rates, cur_s, precision=HIGH)
        cur_v = jnp.where(live, cur_v + H_CHEM * (rates * prod_v), cur_v)
        cur_s = jnp.where(live, cur_s + H_CHEM * (rates * prod_s), cur_s)
        return (cur_v, cur_s)

    flat_v, flat_s = lax.fori_loop(0, trips, substep, (flat_v, flat_s))
    return (flat_v.reshape(num_levels, rows, width), flat_s.reshape(num_species, rows, width))


def local(
    flow, vib, species, field_rate, substeps, vib_rates, kin_rates, level_energy, formation_heat
):
    counts = substeps[:, 0]
    half = flow.shape[1] // 2
    bit = 0
    lent = from_partner(
        (vib[:, half:], species[:, half:], field_rate[half:], counts[half:].astype(jnp.float32)),
        "gy",
        bit,
    )
    work_v = jnp.concatenate([vib[:, :half], lent[0]], 1)
    work_s = jnp.concatenate([species[:, :half], lent[1]], 1)
    work_rate = jnp.concatenate([field_rate[:half], lent[2]], 0)
    work_counts = jnp.concatenate([counts[:half], lent[3].astype(jnp.int32)], 0)
    done_v, done_s = react(work_v, work_s, work_rate, work_counts, vib_rates, kin_rates)
    returned = from_partner((done_v[:, half:], done_s[:, half:]), "gy", bit)
    vib_final = jnp.concatenate([done_v[:, :half], returned[0]], 1)
    species_final = jnp.concatenate([done_s[:, :half], returned[1]], 1)
    heat = jnp.einsum("l,lxy->xy", level_energy, vib - vib_final, precision=HIGH)
    heat = heat + jnp.einsum("l,lxy->xy", formation_heat, species - species_final, precision=HIGH)
    heated = jnp.concatenate([flow[:4], (flow[4] + heat)[None]], 0)
    padded = padded_2(heated, (("gx", 1), ("gy", 2)), 3)
    return (advance(padded), vib_final, species_final)


def solution(mesh):
    return jax.shard_map(
        local,
        mesh=mesh,
        in_specs=(
            P(None, "gx", "gy"),
            P(None, "gx", "gy"),
            P(None, "gx", "gy"),
            P("gx", "gy"),
            P("gx", "gy"),
            P(),
            P(),
            P(),
            P(),
        ),
        out_specs=(P(None, "gx", "gy"), P(None, "gx", "gy"), P(None, "gx", "gy")),
        check_vma=False,
    )
```

profile of v0, /device:TPU:23, one launch (start us, length us, event | category | flops | bytes accessed | tf_op | source)
XLA Modules:
  0.0 175.7 jit_solution(15700517576396754427)
XLA Ops:
  0.7 1.5 slice_bitcast_fusion
  2.1 3.5 %collective-permute-start.2 = (f32[32]{0:T(128)S(1)}, f32[32]{0:T(128)S(1)}, u32[]{:S(2)}, u32[]{:S(2)}) collective-permute-start(f32[32]{0:T(128)S(1)} %get-tuple-element.121), channel_id=1, source_target_pairs={{0,1},{1,0},{2,3},{3,2},{4,5},{5,4},{6,7},{7,6},{8,9},{9,8},{10,11... | collective-permute-start | bytes 392 | tf_op jit(solution)/shard_map/ppermute | solution.py:16
  5.7 2.3 %fusion.36 = (f32[46,32,128]{2,1,0:T(8,128)S(1)}, f32[46,32,128]{2,1,0:T(8,128)}) fusion(f32[46,64,128]{2,1,0:T(8,128)} %param.12), kind=kLoop, calls=%fused_computation.112 | loop fusion | bytes 3014656 | tf_op jit(solution)/shard_map/slice | solution.py:120
  8.0 2.0 %collective-permute-start = (f32[46,32,128]{2,1,0:T(8,128)}, f32[46,32,128]{2,1,0:T(8,128)}, u32[]{:S(2)}, u32[]{:S(2)}) collective-permute-start(f32[46,32,128]{2,1,0:T(8,128)} %get-tuple-element.98), channel_id=1, source_target_pairs={{0,1},{1,0},{2,3},{3,2},{4,5},{5,4},{6,7},{7,6},{8,9},{9,8},{10,11... | collective-permute-start | bytes 2261000 | tf_op jit(solution)/shard_map/ppermute | solution.py:16
  10.1 3.4 %collective-permute-start.1 = (f32[30,32,128]{2,1,0:T(8,128)S(1)}, f32[30,32,128]{2,1,0:T(8,128)S(1)}, u32[]{:S(2)}, u32[]{:S(2)}) collective-permute-start(f32[30,32,128]{2,1,0:T(8,128)S(1)} %get-tuple-element.102), channel_id=1, source_target_pairs={{0,1},{1,0},{2,3},{3,2},{4,5},{5,4},{6,7},{7,6},{8,9},{9,8},{10,11... | collective-permute-start | bytes 1474568 | tf_op jit(solution)/shard_map/ppermute | solution.py:16
  13.5 1.9 %collective-permute-start.3 = (f32[32,128]{1,0:T(8,128)S(1)}, f32[32,128]{1,0:T(8,128)S(1)}, u32[]{:S(2)}, u32[]{:S(2)}) collective-permute-start(f32[32,128]{1,0:T(8,128)S(1)} %get-tuple-element.119), channel_id=1, source_target_pairs={{0,1},{1,0},{2,3},{3,2},{4,5},{5,4},{6,7},{7,6},{8,9},{9,8},{10,11... | collective-permute-start | bytes 49160 | tf_op jit(solution)/shard_map/ppermute | solution.py:16
  15.5 0.6 convert_reduce_fusion
  17.4 21.1 %collective-permute-done.3 = f32[32,128]{1,0:T(8,128)S(1)} collective-permute-done((f32[32,128]{1,0:T(8,128)S(1)}, f32[32,128]{1,0:T(8,128)S(1)}, u32[]{:S(2)}, u32[]{:S(2)}) %collective-permute-start.3) | collective-permute-done | bytes 16416 | tf_op jit(solution)/shard_map/ppermute | solution.py:16
  38.7 0.6 copy.17
  39.3 1.2 pad_maximum_fusion
  40.8 0.9 copy.16
  41.7 49.7 %while.13 = (s32[]{:T(128)}, f32[46,8192]{1,0:T(8,128)S(1)}, f32[30,8192]{1,0:T(8,128)S(1)}, s32[]{:T(128)}, f32[64,128]{1,0:T(8,128)S(1)}, /*index=5*/f32[46,46...) while((s32[]{:T(128)}, f32[46,8192]{1,0:T(8,128)S(1)}, f32[30,8192]{1,0:T(8,128)S(1)}, ...), condition=%wide.region_3.4_spmd.clone, body=%wide.region_2.3_spmd.clone.sunk | while | flops 298983424 | bytes 10064001 | solution.py:105
  41.9 1.7 fusion.56
  43.7 1.1 fusion.57
  45.0 1.7 fusion.56
  46.8 1.1 fusion.57
  48.1 1.7 fusion.56
  49.9 1.1 fusion.57
  51.2 1.7 fusion.56
  53.0 1.1 fusion.57
  54.3 1.7 fusion.56
  56.1 1.1 fusion.57
  57.4 1.7 fusion.56
  59.2 1.1 fusion.57
  60.6 1.7 fusion.56
  62.3 1.1 fusion.57
  63.7 1.7 fusion.56
  65.4 1.1 fusion.57
  66.8 1.7 fusion.56
  68.5 1.1 fusion.57
  69.9 1.7 fusion.56
  71.6 1.1 fusion.57
  73.0 1.7 fusion.56
  74.7 1.1 fusion.57
  76.1 1.7 fusion.56
  77.8 1.1 fusion.57
  79.2 1.7 fusion.56
  80.9 1.1 fusion.57
  82.3 1.7 fusion.56
  84.0 1.1 fusion.57
  85.4 1.7 fusion.56
  87.1 1.1 fusion.57
  88.5 1.7 fusion.56
  90.3 1.1 fusion.57
  91.4 0.2 copy.19
  91.7 2.1 %collective-permute-start.5 = (f32[30,32,128]{2,1,0:T(8,128)S(1)}, f32[30,32,128]{2,1,0:T(8,128)S(1)}, u32[]{:S(2)}, u32[]{:S(2)}) collective-permute-start(f32[30,32,128]{2,1,0:T(8,128)S(1)} %get-tuple-element.100), channel_id=1, source_target_pairs={{0,1},{1,0},{2,3},{3,2},{4,5},{5,4},{6,7},{7,6},{8,9},{9,8},{10,11... | collective-permute-start | bytes 1474568 | tf_op jit(solution)/shard_map/ppermute | solution.py:16
  93.8 0.3 copy.18
  94.2 3.3 %collective-permute-start.4 = (f32[46,32,128]{2,1,0:T(8,128)S(1)}, f32[46,32,128]{2,1,0:T(8,128)S(1)}, u32[]{:S(2)}, u32[]{:S(2)}) collective-permute-start(f32[46,32,128]{2,1,0:T(8,128)S(1)} %get-tuple-element.96), channel_id=1, source_target_pairs={{0,1},{1,0},{2,3},{3,2},{4,5},{5,4},{6,7},{7,6},{8,9},{9,8},{10,11... | collective-permute-start | bytes 2261000 | tf_op jit(solution)/shard_map/ppermute | solution.py:16
  97.5 6.9 %collective-permute-done.5 = f32[30,32,128]{2,1,0:T(8,128)S(1)} collective-permute-done((f32[30,32,128]{2,1,0:T(8,128)S(1)}, f32[30,32,128]{2,1,0:T(8,128)S(1)}, u32[]{:S(2)}, u32[]{:S(2)}) %collective-permute-start.5) | collective-permute-done | bytes 491552 | tf_op jit(solution)/shard_map/ppermute | solution.py:16
  104.4 1.1 fusion.33
  105.5 1.3 fusion.10
  106.8 13.7 %collective-permute-done.4 = f32[46,32,128]{2,1,0:T(8,128)S(1)} collective-permute-done((f32[46,32,128]{2,1,0:T(8,128)S(1)}, f32[46,32,128]{2,1,0:T(8,128)S(1)}, u32[]{:S(2)}, u32[]{:S(2)}) %collective-permute-start.4) | collective-permute-done | bytes 753696 | tf_op jit(solution)/shard_map/ppermute | solution.py:16
  120.6 1.4 fusion.34
  122.0 1.9 %fusion.8 = f32[1,64,128]{2,0,1:T(1,128)S(1)} fusion(f32[46,64,128]{2,1,0:T(8,128)S(1)} %get-tuple-element.93, f32[46]{0:T(128)S(1)} %copy-done.8), kind=kOutput, calls=%fused_computation.10 | convolution fusion | flops 4521984 | bytes 1540280 | tf_op jit(solution)/shard_map/l,lxy->xy/dot_general | solution.py:128
  123.9 17.1 %collective-permute-start.6 = (f32[5,3,128]{2,1,0:T(4,128)S(1)}, f32[5,3,128]{2,1,0:T(4,128)S(1)}, u32[]{:S(2)}, u32[]{:S(2)}) collective-permute-start(f32[5,3,128]{2,1,0:T(4,128)S(1)} %get-tuple-element.116), channel_id=1, source_target_pairs={{0,32},{32,64},{64,96},{96,128},{128,160},{160,192},{192,224},{224... | collective-permute-start | bytes 23048 | tf_op jit(solution)/shard_map/ppermute | solution.py:26
  141.0 1.9 %collective-permute-start.7 = (f32[5,3,128]{2,1,0:T(4,128)S(1)}, f32[5,3,128]{2,1,0:T(4,128)S(1)}, u32[]{:S(2)}, u32[]{:S(2)}) collective-permute-start(f32[5,3,128]{2,1,0:T(4,128)S(1)} %get-tuple-element.117), channel_id=1, source_target_pairs={{32,0},{64,32},{96,64},{128,96},{160,128},{192,160},{224,192},{256... | collective-permute-start | bytes 23048 | tf_op jit(solution)/shard_map/ppermute | solution.py:27
  143.0 14.0 %collective-permute-done.7 = f32[5,3,128]{2,1,0:T(4,128)S(1)} collective-permute-done((f32[5,3,128]{2,1,0:T(4,128)S(1)}, f32[5,3,128]{2,1,0:T(4,128)S(1)}, u32[]{:S(2)}, u32[]{:S(2)}) %collective-permute-start.7) | collective-permute-done | bytes 7712 | tf_op jit(solution)/shard_map/ppermute | solution.py:27
  157.1 2.8 %collective-permute-start.8 = (f32[5,70,3]{2,1,0:T(8,128)S(1)}, f32[5,70,3]{2,1,0:T(8,128)S(1)}, u32[]{:S(2)}, u32[]{:S(2)}) collective-permute-start(f32[5,70,3]{2,1,0:T(8,128)S(1)} %get-tuple-element.108), channel_id=1, source_target_pairs={{0,1},{1,2},{2,3},{3,4},{4,5},{5,6},{6,7},{7,8},{8,9},{9,10},{10,1... | collective-permute-start | bytes 12608 | tf_op jit(solution)/shard_map/ppermute | solution.py:26
  159.9 10.2 %collective-permute-start.9 = (f32[5,70,3]{2,1,0:T(8,128)S(1)}, f32[5,70,3]{2,1,0:T(8,128)S(1)}, u32[]{:S(2)}, u32[]{:S(2)}) collective-permute-start(f32[5,70,3]{2,1,0:T(8,128)S(1)} %get-tuple-element.109), channel_id=1, source_target_pairs={{1,0},{2,1},{3,2},{4,3},{5,4},{6,5},{7,6},{8,7},{9,8},{10,9},{11,1... | collective-permute-start | bytes 12608 | tf_op jit(solution)/shard_map/ppermute | solution.py:27
  170.2 1.0 divide_add_fusion.1
  171.3 1.1 collective-permute-done.9
  172.4 0.2 fusion.14
  173.0 1.8 %divide_add_fusion = f32[5,129,64]{1,2,0:T(8,128)S(1)} fusion(f32[5,134,64]{1,2,0:T(8,128)S(1)} %pad_maximum_fusion.9, f32[5,134,64]{1,2,0:T(8,128)S(1)} %get-tuple-element.103, f32[129,64]{0,1:T(8,128)S(1)} %fusion.26), kind=kLoop, calls=%fused_computation.33 | loop fusion | flops 6068160 | bytes 2179584 | tf_op jit(solution)/shard_map/add | solution.py:70
  174.9 0.7 fusion.23
  (104 shorter events, 5.4 us)
Async XLA Ops:
  0.6 104.9 %copy-start = (f32[30]{0:T(128)S(1)}, f32[30]{0:T(128)}, u32[]{:S(2)}) copy-start(f32[30]{0:T(128)} %param.19) | copy-start | bytes 364
  0.6 9.4 %copy-start.2 = (f32[30,64,128]{2,1,0:T(8,128)S(1)}, f32[30,64,128]{2,1,0:T(8,128)}, u32[]{:S(2)}) copy-start(f32[30,64,128]{2,1,0:T(8,128)} %param.13) | copy-start | bytes 2949124
  2.1 13.3 %collective-permute-start.2 = (f32[32]{0:T(128)S(1)}, f32[32]{0:T(128)S(1)}, u32[]{:S(2)}, u32[]{:S(2)}) collective-permute-start(f32[32]{0:T(128)S(1)} %get-tuple-element.121), channel_id=1, source_target_pairs={{0,1},{1,0},{2,3},{3,2},{4,5},{5,4},{6,7},{7,6},{8,9},{9,8},{10,11... | collective-permute-start | bytes 392 | tf_op jit(solution)/shard_map/ppermute | solution.py:16
  8.0 5.5 %copy-start.7 = (f32[64,128]{1,0:T(8,128)S(1)}, f32[64,128]{1,0:T(8,128)}, u32[]{:S(2)}) copy-start(f32[64,128]{1,0:T(8,128)} %param.14) | copy-start | bytes 98308
  8.0 31.3 %collective-permute-start = (f32[46,32,128]{2,1,0:T(8,128)}, f32[46,32,128]{2,1,0:T(8,128)}, u32[]{:S(2)}, u32[]{:S(2)}) collective-permute-start(f32[46,32,128]{2,1,0:T(8,128)} %get-tuple-element.98), channel_id=1, source_target_pairs={{0,1},{1,0},{2,3},{3,2},{4,5},{5,4},{6,7},{7,6},{8,9},{9,8},{10,11... | collective-permute-start | bytes 2261000 | tf_op jit(solution)/shard_map/ppermute | solution.py:16
  10.1 28.4 %collective-permute-start.1 = (f32[30,32,128]{2,1,0:T(8,128)S(1)}, f32[30,32,128]{2,1,0:T(8,128)S(1)}, u32[]{:S(2)}, u32[]{:S(2)}) collective-permute-start(f32[30,32,128]{2,1,0:T(8,128)S(1)} %get-tuple-element.102), channel_id=1, source_target_pairs={{0,1},{1,0},{2,3},{3,2},{4,5},{5,4},{6,7},{7,6},{8,9},{9,8},{10,11... | collective-permute-start | bytes 1474568 | tf_op jit(solution)/shard_map/ppermute | solution.py:16
  13.5 25.0 %collective-permute-start.3 = (f32[32,128]{1,0:T(8,128)S(1)}, f32[32,128]{1,0:T(8,128)S(1)}, u32[]{:S(2)}, u32[]{:S(2)}) collective-permute-start(f32[32,128]{1,0:T(8,128)S(1)} %get-tuple-element.119), channel_id=1, source_target_pairs={{0,1},{1,0},{2,3},{3,2},{4,5},{5,4},{6,7},{7,6},{8,9},{9,8},{10,11... | collective-permute-start | bytes 49160 | tf_op jit(solution)/shard_map/ppermute | solution.py:16
  40.8 0.9 copy-start.4
  40.8 0.9 copy-start.5
  91.7 12.8 %collective-permute-start.5 = (f32[30,32,128]{2,1,0:T(8,128)S(1)}, f32[30,32,128]{2,1,0:T(8,128)S(1)}, u32[]{:S(2)}, u32[]{:S(2)}) collective-permute-start(f32[30,32,128]{2,1,0:T(8,128)S(1)} %get-tuple-element.100), channel_id=1, source_target_pairs={{0,1},{1,0},{2,3},{3,2},{4,5},{5,4},{6,7},{7,6},{8,9},{9,8},{10,11... | collective-permute-start | bytes 1474568 | tf_op jit(solution)/shard_map/ppermute | solution.py:16
  94.1 3.5 %copy-start.6 = (f32[5,64,128]{2,1,0:T(8,128)S(1)}, f32[5,64,128]{2,1,0:T(8,128)}, u32[]{:S(2)}) copy-start(f32[5,64,128]{2,1,0:T(8,128)} %param.11) | copy-start | bytes 491524
  94.1 10.3 %copy-start.3 = (f32[30,64,128]{2,1,0:T(8,128)S(1)}, f32[30,64,128]{2,1,0:T(8,128)}, u32[]{:S(2)}) copy-start(f32[30,64,128]{2,1,0:T(8,128)} %param.13) | copy-start | bytes 2949124
  94.2 26.4 %collective-permute-start.4 = (f32[46,32,128]{2,1,0:T(8,128)S(1)}, f32[46,32,128]{2,1,0:T(8,128)S(1)}, u32[]{:S(2)}, u32[]{:S(2)}) collective-permute-start(f32[46,32,128]{2,1,0:T(8,128)S(1)} %get-tuple-element.96), channel_id=1, source_target_pairs={{0,1},{1,0},{2,3},{3,2},{4,5},{5,4},{6,7},{7,6},{8,9},{9,8},{10,11... | collective-permute-start | bytes 2261000 | tf_op jit(solution)/shard_map/ppermute | solution.py:16
  104.4 16.1 %copy-start.1 = (f32[46,64,128]{2,1,0:T(8,128)S(1)}, f32[46,64,128]{2,1,0:T(8,128)}, u32[]{:S(2)}) copy-start(f32[46,64,128]{2,1,0:T(8,128)} %param.12) | copy-start | bytes 4521988
  120.6 1.4 copy-start.8
  123.9 19.0 %collective-permute-start.6 = (f32[5,3,128]{2,1,0:T(4,128)S(1)}, f32[5,3,128]{2,1,0:T(4,128)S(1)}, u32[]{:S(2)}, u32[]{:S(2)}) collective-permute-start(f32[5,3,128]{2,1,0:T(4,128)S(1)} %get-tuple-element.116), channel_id=1, source_target_pairs={{0,32},{32,64},{64,96},{96,128},{128,160},{160,192},{192,224},{224... | collective-permute-start | bytes 23048 | tf_op jit(solution)/shard_map/ppermute | solution.py:26
  141.0 15.9 %collective-permute-start.7 = (f32[5,3,128]{2,1,0:T(4,128)S(1)}, f32[5,3,128]{2,1,0:T(4,128)S(1)}, u32[]{:S(2)}, u32[]{:S(2)}) collective-permute-start(f32[5,3,128]{2,1,0:T(4,128)S(1)} %get-tuple-element.117), channel_id=1, source_target_pairs={{32,0},{64,32},{96,64},{128,96},{160,128},{192,160},{224,192},{256... | collective-permute-start | bytes 23048 | tf_op jit(solution)/shard_map/ppermute | solution.py:27
  157.1 14.2 %collective-permute-start.8 = (f32[5,70,3]{2,1,0:T(8,128)S(1)}, f32[5,70,3]{2,1,0:T(8,128)S(1)}, u32[]{:S(2)}, u32[]{:S(2)}) collective-permute-start(f32[5,70,3]{2,1,0:T(8,128)S(1)} %get-tuple-element.108), channel_id=1, source_target_pairs={{0,1},{1,2},{2,3},{3,4},{4,5},{5,6},{6,7},{7,8},{8,9},{9,10},{10,1... | collective-permute-start | bytes 12608 | tf_op jit(solution)/shard_map/ppermute | solution.py:26
  159.9 12.4 %collective-permute-start.9 = (f32[5,70,3]{2,1,0:T(8,128)S(1)}, f32[5,70,3]{2,1,0:T(8,128)S(1)}, u32[]{:S(2)}, u32[]{:S(2)}) collective-permute-start(f32[5,70,3]{2,1,0:T(8,128)S(1)} %get-tuple-element.109), channel_id=1, source_target_pairs={{1,0},{2,1},{3,2},{4,3},{5,4},{6,5},{7,6},{8,7},{9,8},{10,9},{11,1... | collective-permute-start | bytes 12608 | tf_op jit(solution)/shard_map/ppermute | solution.py:27
where the time goes:
time: 176 us
  waiting for transfers between devices  56.8 us (32%)
  starting transfers between devices  48.3 us (27%)
  matrix products  48.1 us (27%)
  other arithmetic  11.6 us (7%)
  local copies, waits for them, and re-layouts  7.8 us (4%)
  between operations  2.34 us (1%)
    ppermute x6, waiting for transfers between devices, from_partner(): return lax.ppermute(value, axis, pairs)  41.7 us
    dot_general x16, matrix products, substep(): prod_v = jnp.dot(vib_rates, cur_v, precision=HIGH)  27 us
    ppermute x2, starting transfers between devices, padded_2(): before = lax.ppermute(last, axis, up)  19.9 us
    dot_general x16, matrix products, substep(): prod_s = jnp.dot(kin_rates, cur_s, precision=HIGH)  17.9 us
    ppermute x6, starting transfers between devices, from_partner(): return lax.ppermute(value, axis, pairs)  16.3 us
    ppermute x2, waiting for transfers between devices, padded_2(): after = lax.ppermute(leading, axis, down)  15.1 us
    ppermute x2, starting transfers between devices, padded_2(): after = lax.ppermute(leading, axis, down)  12.1 us
  transfers between devices with their start and end apart: 10, of which 5 were waited for; matrix products, arithmetic and copies ran while one was open for 4% of the time, Pallas kernels for 0%

commit v1 on v0

v1 whole, which is shorter than its diff:
```python
import jax
import jax.numpy as jnp
from jax import lax
from jax.experimental import pallas as pl
from jax.experimental.pallas import tpu as pltpu
from jax.sharding import PartitionSpec as P

F32, BF16 = jnp.float32, jnp.bfloat16
HIGH = lax.Precision.HIGHEST
VO = (0, 8, 16, 24, 32, 38)
SO = (0, 8, 16, 22)
R = 8


def widen_rates(vr_ref, kr_ref, va, sa):
    va[...] = jnp.zeros_like(va)
    sa[...] = jnp.zeros_like(sa)
    va[0:40, 0:46] = vr_ref[0:40, :]
    va[40:48, 0:46] = vr_ref[38:46, :]
    sa[0:24, 0:30] = kr_ref[0:24, :]
    sa[24:32, 0:30] = kr_ref[22:30, :]
    v = va[...]
    s = sa[...]
    lane = lax.broadcasted_iota(jnp.int32, (48, 128), 1)
    v = jnp.where(lane < 38, v, jnp.where((lane >= 40) & (lane < 48), pltpu.roll(v, 2, 1), 0.0))
    lane = lax.broadcasted_iota(jnp.int32, (32, 128), 1)
    s = jnp.where(
        (lane >= 48) & (lane < 70),
        pltpu.roll(s, 48, 1),
        jnp.where((lane >= 72) & (lane < 80), pltpu.roll(s, 50, 1), 0.0),
    )
    b = jnp.concatenate([v, s, jnp.zeros((48, 128), F32)], 0)
    row = lax.broadcasted_iota(jnp.int32, (128, 128), 0)
    col = lax.broadcasted_iota(jnp.int32, (128, 128), 1)
    rid = jnp.where(row < 40, row, jnp.where(row < 48, row - 2, jnp.where(row < 72, row + 52, row + 50)))
    cid = jnp.where(
        col < 38,
        col,
        jnp.where(
            (col >= 40) & (col < 48),
            col - 2,
            jnp.where((col >= 48) & (col < 70), col + 52, jnp.where((col >= 72) & (col < 80), col + 50, -1)),
        ),
    )
    return b + jnp.where((rid == cid) & (row < 80), 2.0, 0.0)


def pack_split(m):
    hi = m.astype(BF16).astype(F32)
    lo = m - hi
    lane = lax.broadcasted_iota(jnp.int32, m.shape, 1)
    first = jnp.where(lane < 80, hi, pltpu.roll(hi, 80, 1))
    second = jnp.where(lane < 32, pltpu.roll(hi, 80, 1), pltpu.roll(lo, 32, 1))
    return jnp.concatenate([first, second], 1).astype(BF16)


def powers(vr_ref, kr_ref, va, sa, w_scr, w8_scr):
    def mm(a, b):
        return jnp.dot(a, b, precision=HIGH, preferred_element_type=F32)

    b1 = widen_rates(vr_ref, kr_ref, va, sa)
    b2 = mm(b1, b1)
    b3 = mm(b2, b1)
    b4 = mm(b2, b2)
    b5 = mm(b4, b1)
    b6 = mm(b4, b2)
    b7 = mm(b4, b3)
    b8 = mm(b4, b4)
    for j, m in enumerate((b1, b2, b3, b4, b5, b6, b7, b8)):
        w_scr[80 * j : 80 * j + 80, :] = pack_split(m[0:80])
    w8_scr[...] = b8[0:80].astype(BF16)


def coefs(rate, n, s_scr):
    hr = 0.05 * rate
    a = 1.0 - 2.0 * hr
    t = hr / a
    s = n * t
    s_scr[0] = s
    for j in range(1, 16):
        s = s * (((n - j) * (1.0 / (j + 1))) * t)
        s_scr[j] = s
    m = n.astype(jnp.int32)
    p = jnp.ones_like(a)
    q = a
    for k in range(5):
        p = jnp.where(((m >> k) & 1) == 1, p * q, p)
        if k < 4:
            q = q * q
    s_scr[16] = p


def chem_kernel(vr_ref, kr_ref, ev_ref, es_ref, vib_ref, sp_ref, rate_ref, cnt_ref, flow_ref,
                vo_ref, so_ref, e_ref, xa_ref, xb_ref, ya_ref, yb_ref, own_ref, va, sa, w_scr, w8_scr, s_scr, p_scr, y_scr, y1_scr):
    @pl.when(pl.program_id(0) == 0)
    def _():
        powers(vr_ref, kr_ref, va, sa, w_scr, w8_scr)

    g = pl.program_id(0)
    row = lax.broadcasted_iota(jnp.int32, (R, 128), 0)
    n = jnp.zeros((R, 128), jnp.int32)
    for r in range(R):
        n = jnp.where(row == r, cnt_ref[g * R + r], n)
    n = n.astype(F32)
    coefs(rate_ref[...], n, s_scr)
    v2 = vib_ref.reshape(46 * R, 128)
    s2 = sp_ref.reshape(30 * R, 128)
    vo2 = vo_ref.reshape(46 * R, 128)
    so2 = so_ref.reshape(30 * R, 128)

    def cf(i, j):
        return jnp.concatenate([s_scr[j - 1, pl.ds(2 * i, 1), :], s_scr[j - 1, pl.ds(2 * i + 1, 1), :]], 1)

    def load(i):
        def col(r):
            return jnp.concatenate(
                [v2[pl.ds(o * R + r, 8, stride=R), :] for o in VO]
                + [s2[pl.ds(o * R + r, 8, stride=R), :] for o in SO], 0)

        return jnp.concatenate([col(2 * i), col(2 * i + 1)], 1)

    def expand(i):
        x = load(i)
        hi = x.astype(BF16)
        lo = (x - hi.astype(F32)).astype(BF16)
        xk = jnp.concatenate([hi, lo, hi, jnp.zeros((16, 256), BF16)], 0)
        p_scr[i % 2] = jnp.dot(w_scr[...], xk, preferred_element_type=F32)

    def combine(i):
        x = load(i)
        y0 = x
        y1 = cf(i, 8) * x
        for j in range(1, 9):
            w = p_scr[i % 2, 80 * (j - 1) : 80 * j, :]
            if j < 8:
                y0 = y0 + cf(i, j) * w
            y1 = y1 + cf(i, 8 + j) * w
        y_scr[i % 2] = y0
        y1_scr[i % 2] = jnp.concatenate([y1.astype(BF16), jnp.zeros((48, 256), BF16)], 0)

    def finish(i):
        z = jnp.dot(w8_scr[...], y1_scr[i % 2], preferred_element_type=F32)
        out = cf(i, 17) * (y_scr[i % 2] + z)
        for h in range(2):
            r = 2 * i + h
            for k, o in enumerate(VO):
                vo2[pl.ds(o * R + r, 8, stride=R), :] = out[8 * k : 8 * k + 8, 128 * h : 128 * h + 128]
            for k, o in enumerate(SO):
                so2[pl.ds(o * R + r, 8, stride=R), :] = out[48 + 8 * k : 56 + 8 * k, 128 * h : 128 * h + 128]

    NP = R // 2
    for i in range(NP + 2):
        if i < NP:
            expand(i)
        if 0 <= i - 2 < NP:
            finish(i - 2)
        if 0 <= i - 1 < NP:
            combine(i - 1)
    acc = flow_ref[4]
    for l in range(46):
        acc = acc + ev_ref[l] * (vib_ref[l] - vo_ref[l])
    for l in range(30):
        acc = acc + es_ref[l] * (sp_ref[l] - so_ref[l])
    e_ref[...] = acc


    q = [flow_ref[0], flow_ref[1], flow_ref[2], flow_ref[3], acc]
    even_x = lax.axis_index("gx") % 2 == 0
    even_y = lax.axis_index("gy") % 2 == 0

    def rows_to(ref, lo):
        for c in range(5):
            ref[3 * c : 3 * c + 3, :] = q[c][lo : lo + 3, :]
        ref[15:16, :] = jnp.ones((1, 128), F32)

    first, last = g == 0, g == pl.num_programs(0) - 1
    pl.when(first & even_x)(lambda: rows_to(xb_ref, 0))
    pl.when(first & ~even_x)(lambda: rows_to(xa_ref, 0))
    pl.when(last & even_x)(lambda: rows_to(xa_ref, R - 3))
    pl.when(last & ~even_x)(lambda: rows_to(xb_ref, R - 3))

    @pl.when(first)
    def _():
        for ref in (ya_ref, yb_ref, own_ref):
            ref[...] = jnp.ones((8, 128), F32)

    lane = lax.broadcasted_iota(jnp.int32, (8, 128), 1)
    left = own_ref[...]
    right = jnp.where(even_y, ya_ref[...], yb_ref[...])
    for c in range(5):
        at = 16 * g + 3 * c
        here = (lane >= at) & (lane < at + 3)
        left = jnp.where(here, pltpu.roll(q[c], at, 1), left)
        right = jnp.where(here, pltpu.roll(q[c], (at + 3) % 128, 1), right)
    own_ref[...] = left
    ya_ref[...] = jnp.where(even_y, right, left)
    yb_ref[...] = jnp.where(even_y, left, right)


def chem(flow, vib, sp, rate, cnt, vr, kr, ev, es, rows=64):
    full = lambda shape: pl.BlockSpec(shape, lambda i: (0,) * len(shape))
    smem = pl.BlockSpec(memory_space=pltpu.SMEM)
    return pl.pallas_call(
        chem_kernel,
        grid=(rows // R,),
        in_specs=[full((46, 46)), full((30, 30)), smem, smem,
                  pl.BlockSpec((46, R, 128), lambda i: (0, i, 0)),
                  pl.BlockSpec((30, R, 128), lambda i: (0, i, 0)),
                  pl.BlockSpec((R, 128), lambda i: (i, 0)),
                  smem,
                  pl.BlockSpec((5, R, 128), lambda i: (0, i, 0))],
        out_specs=[pl.BlockSpec((46, R, 128), lambda i: (0, i, 0)),
                   pl.BlockSpec((30, R, 128), lambda i: (0, i, 0)),
                   pl.BlockSpec((R, 128), lambda i: (i, 0)),
                   full((16, 128)), full((16, 128)), full((8, 128)), full((8, 128)), full((8, 128))],
        out_shape=[jax.ShapeDtypeStruct((46, rows, 128), F32), jax.ShapeDtypeStruct((30, rows, 128), F32),
                   jax.ShapeDtypeStruct((rows, 128), F32)]
        + [jax.ShapeDtypeStruct((k, 128), F32) for k in (16, 16, 8, 8, 8)],
        scratch_shapes=[pltpu.VMEM((48, 128), F32), pltpu.VMEM((32, 128), F32),
                        pltpu.VMEM((640, 256), BF16), pltpu.VMEM((80, 128), BF16),
                        pltpu.VMEM((17, R, 128), F32), pltpu.VMEM((2, 640, 256), F32),
                        pltpu.VMEM((2, 80, 256), F32), pltpu.VMEM((2, 128, 256), BF16)],
        compiler_params=pltpu.CompilerParams(vmem_limit_bytes=62 * 2**20),
        cost_estimate=pl.CostEstimate(flops=10**9, bytes_accessed=6 * 10**6, transcendentals=0),
        name="chemistry",
    )(vr, kr, ev, es, vib, sp, rate, cnt, flow)


def cell_flux(q, d):
    inv = 1.0 / q[0]
    u = q[d] * inv
    p = 0.4 * (q[4] - 0.5 * (q[1] * q[1] + q[2] * q[2] + q[3] * q[3]) * inv)
    f = [q[0] * u, q[1] * u, q[2] * u, q[3] * u, (q[4] + p) * u]
    f[d] = f[d] + p
    return f, jnp.abs(u) + jnp.sqrt(1.4 * p * inv)


def recip(v):
    return pl.reciprocal(v, approx=True)


def side(v2, d0, d1, d2, d3):
    c0, c1, c2 = d1 - d0, d2 - d1, d3 - d2
    t1 = 3.0 * d1
    e0 = t1 - d0
    e1 = d1 + d2
    e2 = d3 - 3.0 * d2
    k = 13.0 / 3.0
    s0 = 1.6e-5 + (k * (c0 * c0) + e0 * e0)
    s1 = 1.6e-5 + (k * (c1 * c1) + e1 * e1)
    s2 = 1.6e-5 + (k * (c2 * c2) + e2 * e2)
    r0, r1, r2 = recip(s0), recip(s1), recip(s2)
    a0 = r0 * r0
    a1 = 6.0 * (r1 * r1)
    a2 = 3.0 * (r2 * r2)
    num = a0 * ((c0 + c0) + t1) + a1 * (e1 + d2) + a2 * (d2 - e2)
    den = a0 + a1 + a2
    return v2 + num / (6.0 * den)


def face(f, q, alpha):
    fd = [f[k + 1] - f[k] for k in range(5)]
    qd = [alpha * (q[k + 1] - q[k]) for k in range(5)]
    plus = side(f[2] + alpha * q[2], *[fd[k] + qd[k] for k in range(4)])
    m = [qd[k] - fd[k] for k in range(5)]
    minus = side(f[3] - alpha * q[3], m[4], m[3], m[2], m[1])
    return plus + minus


def weno_kernel(flow_ref, e_ref, xa_ref, xb_ref, ya_ref, yb_ref, own_ref, out_ref, xq, xf, xs, xg):
    even_x = lax.axis_index("gx") % 2 == 0
    even_y = lax.axis_index("gy") % 2 == 0
    xa, xb, ya, yb = xa_ref[...], xb_ref[...], ya_ref[...], yb_ref[...]
    up, dn = jnp.where(even_x, xb, xa), jnp.where(even_x, xa, xb)
    lq, rq = jnp.where(even_y, yb, ya), jnp.where(even_y, ya, yb)
    for c in range(5):
        xq[c, 5:8, :] = up[3 * c : 3 * c + 3, :]
        xq[c, 8:72, :] = e_ref[...] if c == 4 else flow_ref[c]
        xq[c, 72:75, :] = dn[3 * c : 3 * c + 3, :]
    one = jnp.ones((5, 128), F32)
    for c in range(5):
        fill = one if c in (0, 4) else 0.0 * one
        xq[c, 0:5, :] = fill
        xq[c, 75:80, :] = fill
    for g in range(10):
        sl = slice(8 * g, 8 * g + 8)
        f, s = cell_flux([xq[c, sl, :] for c in range(5)], 1)
        for c in range(5):
            xf[c, sl, :] = f[c]
        xs[sl, :] = s
    for g in range(9):
        b = 8 * g + 5
        n = 8 if g < 8 else 1
        alpha = xs[b : b + n, :]
        for o in range(1, 6):
            alpha = jnp.maximum(alpha, xs[b + o : b + o + n, :])
        for c in range(5):
            xg[c, 8 * g : 8 * g + n, :] = face(
                [xf[c, b + o : b + o + n, :] for o in range(6)],
                [xq[c, b + o : b + o + n, :] for o in range(6)],
                alpha,
            )

    lane = lax.broadcasted_iota(jnp.int32, (8, 128), 1)
    slot = lane % 16

    def shift(v, k):
        return v if k % 128 == 0 else pltpu.roll(v, (-k) % 128, 1)

    def strip(v):
        q = [shift(v, 3 * c) for c in range(5)]
        f, s = cell_flux(q, 2)
        ff = f[0]
        ss = s
        for c in range(1, 5):
            here = slot >= 3 * c
            ff = jnp.where(here, shift(f[c], -3 * c), ff)
            ss = jnp.where(here, shift(s, -3 * c), ss)
        return v, ff, ss

    lq, lfx, ls = strip(lq)
    oq, ofx, os_ = strip(own_ref[...])
    alpha = ls
    for v in (shift(ls, 1), shift(ls, 2), os_, shift(os_, 1), shift(os_, 2)):
        alpha = jnp.maximum(alpha, v)
    first = face(
        [lfx, shift(lfx, 1), shift(lfx, 2), ofx, shift(ofx, 1), shift(ofx, 2)],
        [lq, shift(lq, 1), shift(lq, 2), oq, shift(oq, 1), shift(oq, 2)],
        alpha,
    )
    for g in range(8):
        sl = slice(8 * g + 8, 8 * g + 16)
        q = [xq[c, sl, :] for c in range(5)]
        h = [
            jnp.where(lane < 64, shift(rq, 16 * g + 3 * c), shift(lq, 16 * g + 3 * c - 125)) for c in range(5)
        ]
        f, s = cell_flux(q, 2)
        hf, hs = cell_flux(h, 2)

        def six(a, b):
            out = []
            for o in range(-2, 4):
                if o == 0:
                    out.append(a)
                elif o > 0:
                    out.append(shift(jnp.where(lane < o, b, a), o))
                else:
                    out.append(shift(jnp.where(lane >= 128 + o, b, a), o))
            return out

        alphas = six(s, hs)
        alpha = alphas[0]
        for v in alphas[1:]:
            alpha = jnp.maximum(alpha, v)
        for c in range(5):
            after = face(six(f[c], hf[c]), six(q[c], h[c]), alpha)
            before = jnp.where(lane == 0, shift(first, 16 * g + 3 * c), shift(after, -1))
            gx = xg[c, 8 * g + 1 : 8 * g + 9, :] - xg[c, 8 * g : 8 * g + 8, :]
            out_ref[c, 8 * g : 8 * g + 8, :] = q[c] - 0.05 * (gx + (after - before))


def weno(flow, e, xa, xb, ya, yb, own):
    vm = pl.BlockSpec(memory_space=pltpu.VMEM)
    return pl.pallas_call(
        weno_kernel,
        in_specs=[vm] * 7,
        out_specs=vm,
        out_shape=jax.ShapeDtypeStruct((5, 64, 128), F32),
        scratch_shapes=[pltpu.VMEM((5, 80, 128), F32), pltpu.VMEM((5, 80, 128), F32), pltpu.VMEM((80, 128), F32),
                        pltpu.VMEM((5, 72, 128), F32)],
        compiler_params=pltpu.CompilerParams(vmem_limit_bytes=62 * 2**20),
        cost_estimate=pl.CostEstimate(flops=10**7, bytes_accessed=10**6, transcendentals=0),
        name="euler_weno",
    )(flow, e, xa, xb, ya, yb, own)


def swaps(size, start):
    pairs = [(i % size, (i + 1) % size) for i in range(start, size, 2)]
    return pairs + [(b, a) for a, b in pairs]


def swapped(value, axis, start):
    return lax.ppermute(value, axis, swaps(lax.axis_size(axis), start))


def local(flow, vib, species, field_rate, substeps, vib_rates, kin_rates, level_energy, formation_heat):
    vib_final, species_final, e, xa, xb, ya, yb, own = chem(
        flow, vib, species, field_rate, substeps.reshape(-1), vib_rates, kin_rates, level_energy, formation_heat
    )
    ya = swapped(ya, "gy", 0)
    yb = swapped(yb, "gy", 1)
    xa = swapped(xa, "gx", 0)
    xb = swapped(xb, "gx", 1)
    return (weno(flow, e, xa, xb, ya, yb, own), vib_final, species_final)


def solution(mesh):
    tiled = P(None, "gx", "gy")
    return jax.shard_map(
        local,
        mesh=mesh,
        in_specs=(tiled, tiled, tiled, P("gx", "gy"), P("gx", "gy"), P(), P(), P(), P()),
        out_specs=(tiled, tiled, tiled),
        check_vma=False,
    )
```

time: 176 us -> 54.4 us (0.31)
  the two profiles are of different devices: /device:TPU:23 before, /device:TPU:16 now
where the time goes in v1:
time: 54.4 us; the launch traced here: 54.2 us
  starting transfers between devices  28.4 us (52%)
  Pallas kernels  16.8 us (31%)
  waiting for transfers between devices  7.67 us (14%)
  between operations  0.71 us (1%)
  local copies, waits for them, and re-layouts  0.58 us (1%)
    ppermute x4, starting transfers between devices, swapped(): return lax.ppermute(value, axis, swaps(lax.axis_size(axis), start))  28.4 us
    pallas_call x1, Pallas kernels, chem(): pl.pallas_call(chem_kernel, grid=(rows // R,), in_specs=[full((46, 46)),...  11.6 us
    ppermute x4, waiting for transfers between devices, swapped(): return lax.ppermute(value, axis, swaps(lax.axis_size(axis), start))  7.67 us
    pallas_call x1, Pallas kernels, weno(): pl.pallas_call(weno_kernel, in_specs=[vm] * 7, out_specs=vm, out_shape=ja...  5.28 us
  transfers between devices with their start and end apart: 4, of which 1 were waited for; matrix products, arithmetic and copies ran while one was open for 0% of the time, Pallas kernels for 0%

profile of v1, /device:TPU:16, one launch (start us, length us, event | category | flops | bytes accessed | tf_op | source)
XLA Modules:
  0.0 54.2 jit_solution(7667101864248369056)
XLA Ops:
  0.6 11.6 %chemistry.1 = (f32[46,64,128]{2,1,0:T(8,128)}, f32[30,64,128]{2,1,0:T(8,128)}, f32[64,128]{1,0:T(8,128)}, f32[16,128]{1,0:T(8,128)}, f32[16,128]{1,0:T(8,128)},...) custom-call(f32[46,46]{1,0:T(8,128)} %vr_ref.1, f32[30,30]{1,0:T(8,128)} %kr_ref.1, f32[46]{0:T(128)} %ev_ref.1, ...), custom_call_target="tpu_custom_call" | custom-call | flops 1000000000 | bytes 6000000 | tf_op jit(solution)/shard_map/chemistry/pallas_call | solution.py:203
  12.2 1.9 %collective-permute-start = (f32[16,128]{1,0:T(8,128)}, f32[16,128]{1,0:T(8,128)S(1)}, u32[]{:S(2)}, u32[]{:S(2)}) collective-permute-start(f32[16,128]{1,0:T(8,128)} %get-tuple-element.12), channel_id=1, source_target_pairs={{0,32},{64,96},{128,160},{192,224},{256,288},{320,352},{384,416},{... | collective-permute-start | bytes 24584 | tf_op jit(solution)/shard_map/ppermute | solution.py:383
  14.1 18.0 %collective-permute-start.1 = (f32[16,128]{1,0:T(8,128)}, f32[16,128]{1,0:T(8,128)S(1)}, u32[]{:S(2)}, u32[]{:S(2)}) collective-permute-start(f32[16,128]{1,0:T(8,128)} %get-tuple-element.13), channel_id=1, source_target_pairs={{32,64},{96,128},{160,192},{224,256},{288,320},{352,384},{416,448}... | collective-permute-start | bytes 24584 | tf_op jit(solution)/shard_map/ppermute | solution.py:383
  32.2 2.9 %collective-permute-start.2 = (f32[8,128]{1,0:T(8,128)}, f32[8,128]{1,0:T(8,128)S(1)}, u32[]{:S(2)}, u32[]{:S(2)}) collective-permute-start(f32[8,128]{1,0:T(8,128)} %get-tuple-element.14), channel_id=1, source_target_pairs={{0,1},{2,3},{4,5},{6,7},{8,9},{10,11},{12,13},{14,15},{16,17},{18,... | collective-permute-start | bytes 12296 | tf_op jit(solution)/shard_map/ppermute | solution.py:383
  35.1 5.5 %collective-permute-start.3 = (f32[8,128]{1,0:T(8,128)}, f32[8,128]{1,0:T(8,128)S(1)}, u32[]{:S(2)}, u32[]{:S(2)}) collective-permute-start(f32[8,128]{1,0:T(8,128)} %get-tuple-element.15), channel_id=1, source_target_pairs={{1,2},{3,4},{5,6},{7,8},{9,10},{11,12},{13,14},{15,16},{17,18},{19... | collective-permute-start | bytes 12296 | tf_op jit(solution)/shard_map/ppermute | solution.py:383
  40.6 0.0 collective-permute-done.2.ya_ref
  40.6 0.0 copy-start.2
  40.6 7.7 %collective-permute-done.3.yb_ref = f32[8,128]{1,0:T(8,128)S(1)} collective-permute-done((f32[8,128]{1,0:T(8,128)}, f32[8,128]{1,0:T(8,128)S(1)}, u32[]{:S(2)}, u32[]{:S(2)}) %collective-permute-start.3) | collective-permute-done | bytes 4128 | tf_op jit(solution)/shard_map/ppermute | solution.py:383
  48.3 0.0 copy-start.3
  48.3 0.0 collective-permute-done.xa_ref
  48.3 0.0 copy-start
  48.3 0.0 collective-permute-done.1.xb_ref
  48.3 0.0 copy-start.1
  48.3 0.0 copy-done.2
  48.3 0.6 %copy-done.3 = f32[8,128]{1,0:T(8,128)} copy-done((f32[8,128]{1,0:T(8,128)}, f32[8,128]{1,0:T(8,128)S(1)}, u32[]{:S(2)}) %copy-start.3) | copy-done | bytes 4120
  48.9 0.0 copy-done
  48.9 0.0 copy-done.1
  48.9 5.3 %euler_weno.1 = f32[5,64,128]{2,1,0:T(8,128)} custom-call(f32[5,64,128]{2,1,0:T(8,128)} %flow_ref.3, f32[64,128]{1,0:T(8,128)} %get-tuple-element.11.e_ref, f32[16,128]{1,0:T(8,128)} %copy-done, f32[16,128]{1,0:T(8,128)} %copy-done.1, f32[8,128]{1,0:T(8,128)} %copy-done.2, f32[8,128]{1,0:T(8,128)} %copy-done.3, f32[8,128]{1,0:T(8,128)} %get-tuple-element.16.own_ref), custom_call_target="tpu_custom_call" | custom-call | flops 10000000 | bytes 1000000 | tf_op jit(solution)/shard_map/euler_weno/pallas_call | solution.py:364
Async XLA Ops:
  12.2 36.1 %collective-permute-start = (f32[16,128]{1,0:T(8,128)}, f32[16,128]{1,0:T(8,128)S(1)}, u32[]{:S(2)}, u32[]{:S(2)}) collective-permute-start(f32[16,128]{1,0:T(8,128)} %get-tuple-element.12), channel_id=1, source_target_pairs={{0,32},{64,96},{128,160},{192,224},{256,288},{320,352},{384,416},{... | collective-permute-start | bytes 24584 | tf_op jit(solution)/shard_map/ppermute | solution.py:383
  14.1 34.2 %collective-permute-start.1 = (f32[16,128]{1,0:T(8,128)}, f32[16,128]{1,0:T(8,128)S(1)}, u32[]{:S(2)}, u32[]{:S(2)}) collective-permute-start(f32[16,128]{1,0:T(8,128)} %get-tuple-element.13), channel_id=1, source_target_pairs={{32,64},{96,128},{160,192},{224,256},{288,320},{352,384},{416,448}... | collective-permute-start | bytes 24584 | tf_op jit(solution)/shard_map/ppermute | solution.py:383
  32.2 8.5 %collective-permute-start.2 = (f32[8,128]{1,0:T(8,128)}, f32[8,128]{1,0:T(8,128)S(1)}, u32[]{:S(2)}, u32[]{:S(2)}) collective-permute-start(f32[8,128]{1,0:T(8,128)} %get-tuple-element.14), channel_id=1, source_target_pairs={{0,1},{2,3},{4,5},{6,7},{8,9},{10,11},{12,13},{14,15},{16,17},{18,... | collective-permute-start | bytes 12296 | tf_op jit(solution)/shard_map/ppermute | solution.py:383
  35.1 13.2 %collective-permute-start.3 = (f32[8,128]{1,0:T(8,128)}, f32[8,128]{1,0:T(8,128)S(1)}, u32[]{:S(2)}, u32[]{:S(2)}) collective-permute-start(f32[8,128]{1,0:T(8,128)} %get-tuple-element.15), channel_id=1, source_target_pairs={{1,2},{3,4},{5,6},{7,8},{9,10},{11,12},{13,14},{15,16},{17,18},{19... | collective-permute-start | bytes 12296 | tf_op jit(solution)/shard_map/ppermute | solution.py:383
  40.6 7.7 %copy-start.2 = (f32[8,128]{1,0:T(8,128)}, f32[8,128]{1,0:T(8,128)S(1)}, u32[]{:S(2)}) copy-start(f32[8,128]{1,0:T(8,128)S(1)} %collective-permute-done.2.ya_ref) | copy-start | bytes 12292
  48.3 0.6 %copy-start.3 = (f32[8,128]{1,0:T(8,128)}, f32[8,128]{1,0:T(8,128)S(1)}, u32[]{:S(2)}) copy-start(f32[8,128]{1,0:T(8,128)S(1)} %collective-permute-done.3.yb_ref) | copy-start | bytes 12292
  48.3 0.6 %copy-start = (f32[16,128]{1,0:T(8,128)}, f32[16,128]{1,0:T(8,128)S(1)}, u32[]{:S(2)}) copy-start(f32[16,128]{1,0:T(8,128)S(1)} %collective-permute-done.xa_ref) | copy-start | bytes 24580
  48.3 0.6 %copy-start.1 = (f32[16,128]{1,0:T(8,128)}, f32[16,128]{1,0:T(8,128)S(1)}, u32[]{:S(2)}) copy-start(f32[16,128]{1,0:T(8,128)S(1)} %collective-permute-done.1.xb_ref) | copy-start | bytes 24580

commit v2 on v1

v2 whole, which is shorter than its diff:
```python
import functools

import jax
import jax.numpy as jnp
from jax import lax
from jax.experimental import pallas as pl
from jax.experimental.pallas import tpu as pltpu
from jax.sharding import PartitionSpec as P

F32, BF16 = jnp.float32, jnp.bfloat16
HIGH = lax.Precision.HIGHEST
VO = (0, 8, 16, 24, 32, 38)
SO = (0, 8, 16, 22)


def widen_rates(vr_ref, kr_ref, va, sa):
    va[...] = jnp.zeros_like(va)
    sa[...] = jnp.zeros_like(sa)
    va[0:40, 0:46] = vr_ref[0:40, :]
    va[40:48, 0:46] = vr_ref[38:46, :]
    sa[0:24, 0:30] = kr_ref[0:24, :]
    sa[24:32, 0:30] = kr_ref[22:30, :]
    v = va[...]
    s = sa[...]
    lane = lax.broadcasted_iota(jnp.int32, (48, 128), 1)
    v = jnp.where(lane < 38, v, jnp.where((lane >= 40) & (lane < 48), pltpu.roll(v, 2, 1), 0.0))
    lane = lax.broadcasted_iota(jnp.int32, (32, 128), 1)
    s = jnp.where(
        (lane >= 48) & (lane < 70),
        pltpu.roll(s, 48, 1),
        jnp.where((lane >= 72) & (lane < 80), pltpu.roll(s, 50, 1), 0.0),
    )
    b = jnp.concatenate([v, s, jnp.zeros((48, 128), F32)], 0)
    row = lax.broadcasted_iota(jnp.int32, (128, 128), 0)
    col = lax.broadcasted_iota(jnp.int32, (128, 128), 1)
    rid = jnp.where(row < 40, row, jnp.where(row < 48, row - 2, jnp.where(row < 72, row + 52, row + 50)))
    cid = jnp.where(
        col < 38,
        col,
        jnp.where(
            (col >= 40) & (col < 48),
            col - 2,
            jnp.where((col >= 48) & (col < 70), col + 52, jnp.where((col >= 72) & (col < 80), col + 50, -1)),
        ),
    )
    return b + jnp.where((rid == cid) & (row < 80), 2.0, 0.0)


def pack_split(m):
    hi = m.astype(BF16).astype(F32)
    lo = m - hi
    lane = lax.broadcasted_iota(jnp.int32, m.shape, 1)
    first = jnp.where(lane < 80, hi, pltpu.roll(hi, 80, 1))
    second = jnp.where(lane < 32, pltpu.roll(hi, 80, 1), pltpu.roll(lo, 32, 1))
    return jnp.concatenate([first, second], 1).astype(BF16)


def mm(a, b):
    return jnp.dot(a, b, precision=HIGH, preferred_element_type=F32)


def load_pair(v2, s2, g, k):
    def one(r):
        return jnp.concatenate(
            [v2[pl.ds(g * 368 + (o * 8 + r), 8, stride=8), :] for o in VO]
            + [s2[pl.ds(g * 240 + (o * 8 + r), 8, stride=8), :] for o in SO], 0)

    return jnp.concatenate([one(2 * k), one(2 * k + 1)], 1)


def split_stack(x):
    hi = x.astype(BF16)
    lo = (x - hi.astype(F32)).astype(BF16)
    return jnp.concatenate([hi, lo, hi, jnp.zeros((16, 256), BF16)], 0)


def group_counts(cnt_ref, g):
    row = lax.broadcasted_iota(jnp.int32, (8, 128), 0)
    n = jnp.zeros((8, 128), jnp.int32)
    for r in range(8):
        n = jnp.where(row == r, cnt_ref[g * 8 + r], n)
    return n.astype(F32)


def heat_kernel(vr_hbm, kr_hbm, ev_hbm, es_hbm, cnt_hbm, rate_hbm, flow_hbm, vib_hbm, sp_hbm,
                e_ref, xa_ref, xb_ref, ya_ref, yb_ref, own_ref,
                vr_ref, kr_ref, ev_ref, es_ref, cnt_ref, rate_ref, flow_ref,
                vib, sp, va, sa, ee, g_scr, s_scr, p_scr, w_scr, sems, wsem):
    small = [pltpu.make_async_copy(a, b, wsem.at[k])
             for k, (a, b) in enumerate(((vr_hbm, vr_ref), (kr_hbm, kr_ref), (ev_hbm, ev_ref), (es_hbm, es_ref),
                                         (cnt_hbm, cnt_ref), (rate_hbm, rate_ref), (flow_hbm, flow_ref)))]
    for c in small[:6]:
        c.start()

    def pieces(g):
        sl = pl.ds(pl.multiple_of(8 * g, 8), 8)
        return (pltpu.make_async_copy(vib_hbm.at[:, sl, :], vib.at[g], sems.at[0, g]),
                pltpu.make_async_copy(sp_hbm.at[:, sl, :], sp.at[g], sems.at[1, g]))

    for g in range(8):
        for c in pieces(g):
            c.start()
    small[6].start()
    for c in small[:6]:
        c.wait()
    for g in range(8):
        coefs(rate_ref[8 * g : 8 * g + 8, :], group_counts(cnt_ref, g), s_scr, 8 * g)

    b1 = widen_rates(vr_ref, kr_ref, va, sa)
    ee[...] = jnp.zeros_like(ee)
    ee[0:1, 0:46] = ev_ref[...]
    ee[8:9, 0:30] = es_ref[...]
    lane = lax.broadcasted_iota(jnp.int32, (8, 128), 1)
    v, s = ee[0:8, :], ee[8:16, :]
    v = jnp.where(lane < 38, v, jnp.where((lane >= 40) & (lane < 48), pltpu.roll(v, 2, 1), 0.0))
    v = jnp.where((lane >= 48) & (lane < 70), pltpu.roll(s, 48, 1),
                  jnp.where((lane >= 72) & (lane < 80), pltpu.roll(s, 50, 1), v))
    G = jnp.concatenate([v, jnp.zeros((24, 128), F32)], 0)
    b2 = mm(b1, b1)
    G = G + pltpu.roll(mm(G, b1), 1, 0)
    b4 = mm(b2, b2)
    G = G + pltpu.roll(mm(G, b2), 2, 0)
    b8 = mm(b4, b4)
    G = G + pltpu.roll(mm(G, b4), 4, 0)
    G = G + pltpu.roll(mm(G, b8), 8, 0)
    row = lax.broadcasted_iota(jnp.int32, (32, 128), 0)
    G = G + jnp.where(row == 16, pltpu.roll(mm(G, b8), 8, 0), 0.0)
    g_scr[...] = pack_split(G)

    v2 = vib.reshape(8 * 368, 128)
    s2 = sp.reshape(8 * 240, 128)
    even_x = lax.axis_index("gx") % 2 == 0
    even_y = lax.axis_index("gy") % 2 == 0
    small[6].wait()

    def sums(g, left, right):
        sl = pl.ds(pl.multiple_of(8 * g, 8), 8)
        first = p_scr[pl.ds(192 * g, 8, stride=24), :]
        acc = first
        for j in range(1, 17):
            acc = acc + s_scr[j - 1, sl, :] * p_scr[pl.ds(192 * g + j, 8, stride=24), :]
        e = flow_ref[4, sl, :] + (first - s_scr[16, sl, :] * acc)
        e_ref[sl, :] = e
        for c in range(5):
            at = 16 * g + 3 * c
            v = e if c == 4 else flow_ref[c, sl, :]
            here = (lane >= at) & (lane < at + 3)
            left = jnp.where(here, pltpu.roll(v, at, 1), left)
            right = jnp.where(here, pltpu.roll(v, lax.rem(at + 3, 128), 1), right)
        return left, right

    p_scr[0:192, :] = jnp.zeros((192, 128), F32)

    def turn(g, carry):
        for c in pieces(g):
            c.wait()
        for i in range(4):
            r = 8 * g + 2 * i
            w = jnp.dot(g_scr[...], split_stack(load_pair(v2, s2, g, i)), preferred_element_type=F32)
            w_scr[48 * i : 48 * i + 24, :] = w[0:24, 0:128]
            w_scr[48 * i + 24 : 48 * i + 48, :] = w[0:24, 128:256]
        out = sums(jnp.maximum(g - 1, 0), *carry)
        p_scr[pl.ds(pl.multiple_of(192 * g, 8), 192), :] = w_scr[...]
        return out

    left = jnp.ones((8, 128), F32)
    left, right = lax.fori_loop(0, 8, turn, (left, left))
    left, right = sums(7, left, right)
    edge = {}
    for g in (0, 7):
        sl = slice(8 * g, 8 * g + 8)
        edge[g] = [flow_ref[c, sl, :] for c in range(4)] + [e_ref[sl, :]]
    own_ref[...] = left
    ya_ref[0:8, :] = jnp.where(even_y, right, left)
    yb_ref[0:8, :] = jnp.where(even_y, left, right)
    ya_ref[8:16, :] = jnp.ones((8, 128), F32)
    yb_ref[8:16, :] = jnp.ones((8, 128), F32)
    for c in range(5):
        top, bottom = edge[0][c][0:3, :], edge[7][c][5:8, :]
        xa_ref[3 * c : 3 * c + 3, :] = jnp.where(even_x, bottom, top)
        xb_ref[3 * c : 3 * c + 3, :] = jnp.where(even_x, top, bottom)
    xa_ref[15:16, :] = jnp.ones((1, 128), F32)
    xb_ref[15:16, :] = jnp.ones((1, 128), F32)


def heat(flow, vib, sp, rate, cnt, vr, kr, ev, es):
    vm = pl.BlockSpec(memory_space=pltpu.VMEM)
    hbm = pl.BlockSpec(memory_space=pl.ANY)
    return pl.pallas_call(
        heat_kernel,
        in_specs=[hbm] * 9,
        out_specs=[vm] * 6,
        out_shape=[jax.ShapeDtypeStruct((k, 128), F32) for k in (64, 16, 16, 16, 16, 8)],
        scratch_shapes=[pltpu.VMEM((46, 46), F32), pltpu.VMEM((30, 30), F32), pltpu.VMEM((1, 46), F32),
                        pltpu.VMEM((1, 30), F32), pltpu.SMEM((64,), jnp.int32), pltpu.VMEM((64, 128), F32),
                        pltpu.VMEM((5, 64, 128), F32),
                        pltpu.VMEM((8, 46, 8, 128), F32), pltpu.VMEM((8, 30, 8, 128), F32),
                        pltpu.VMEM((48, 128), F32), pltpu.VMEM((32, 128), F32), pltpu.VMEM((16, 128), F32),
                        pltpu.VMEM((32, 256), BF16), pltpu.VMEM((17, 64, 128), F32), pltpu.VMEM((1536, 128), F32),
                        pltpu.VMEM((192, 128), F32),
                        pltpu.SemaphoreType.DMA((2, 8)), pltpu.SemaphoreType.DMA((7,))],
        compiler_params=pltpu.CompilerParams(vmem_limit_bytes=62 * 2**20),
        cost_estimate=pl.CostEstimate(flops=10**8, bytes_accessed=3 * 10**6, transcendentals=0),
        name="heat",
    )(vr, kr, ev.reshape(1, -1), es.reshape(1, -1), cnt, rate, flow, vib, sp)


def powers(vr_ref, kr_ref, va, sa, w_scr, w8_scr):
    b1 = widen_rates(vr_ref, kr_ref, va, sa)
    b2 = mm(b1, b1)
    b3 = mm(b2, b1)
    b4 = mm(b2, b2)
    b5 = mm(b4, b1)
    b6 = mm(b4, b2)
    b7 = mm(b4, b3)
    b8 = mm(b4, b4)
    for j, m in enumerate((b1, b2, b3, b4, b5, b6, b7, b8)):
        w_scr[80 * j : 80 * j + 80, :] = pack_split(m[0:80])
    w8_scr[...] = b8[0:80].astype(BF16)


def coefs(rate, n, s_scr, at):
    hr = 0.05 * rate
    a = 1.0 - 2.0 * hr
    t = hr / a
    s = n * t
    s_scr[0, at : at + 8, :] = s
    for j in range(1, 16):
        s = s * (((n - j) * (1.0 / (j + 1))) * t)
        s_scr[j, at : at + 8, :] = s
    m = n.astype(jnp.int32)
    p = jnp.ones_like(a)
    q = a
    for k in range(5):
        p = jnp.where(((m >> k) & 1) == 1, p * q, p)
        if k < 4:
            q = q * q
    s_scr[16, at : at + 8, :] = p


def chem_kernel(early, vr_hbm, kr_hbm, cnt_hbm, rate_hbm, vib_hbm, sp_hbm, *rest):
    vo_hbm, so_hbm = rest[4:6] if early else rest[2:4]
    vr, kr, cnt, rate, vib, sp, vo, so, va, sa, w_scr, w8_scr, s_scr, p_scr, y_scr, y1_scr, sems, osems, wsem = rest[-19:]
    half = lax.axis_size("gx") // 2

    @pl.when(((lax.axis_index("gx") < half) & (lax.axis_index("gy") % 8 < 4)) == early)
    def _():
        small = [pltpu.make_async_copy(a, b, wsem.at[k])
                 for k, (a, b) in enumerate(((vr_hbm, vr), (kr_hbm, kr), (rate_hbm, rate), (cnt_hbm, cnt)))]
        for c in small:
            c.start()

        def group(hbm, ref, g, sem, out=False):
            sl = pl.ds(pl.multiple_of(8 * g, 8), 8)
            a, b = hbm.at[:, sl, :], ref.at[g]
            return pltpu.make_async_copy(b, a, sem) if out else pltpu.make_async_copy(a, b, sem)

        for g in range(8):
            group(vib_hbm, vib, g, sems.at[0, g]).start()
            group(sp_hbm, sp, g, sems.at[1, g]).start()
        for c in small:
            c.wait()
        powers(vr, kr, va, sa, w_scr, w8_scr)
        v2 = vib.reshape(8 * 368, 128)
        s2 = sp.reshape(8 * 240, 128)
        vo2 = vo.reshape(8 * 368, 128)
        so2 = so.reshape(8 * 240, 128)

        for g in range(8):
            coefs(rate[8 * g : 8 * g + 8, :], group_counts(cnt, g), s_scr, 8 * g)

        def ready(g):
            group(vib_hbm, vib, g, sems.at[0, g]).wait()
            group(sp_hbm, sp, g, sems.at[1, g]).wait()

        def emit(g):
            group(vo_hbm, vo, g, osems.at[0, g], True).start()
            group(so_hbm, so, g, osems.at[1, g], True).start()

        def cf(g, k, j):
            at = 8 * g + 2 * k
            return jnp.concatenate([s_scr[j - 1, pl.ds(at, 1), :], s_scr[j - 1, pl.ds(at + 1, 1), :]], 1)

        def expand(g, k, slot):
            p_scr[slot] = jnp.dot(w_scr[...], split_stack(load_pair(v2, s2, g, k)), preferred_element_type=F32)

        def combine(g, k, slot):
            x = load_pair(v2, s2, g, k)
            y0 = x
            y1 = cf(g, k, 8) * x
            for j in range(1, 9):
                w = p_scr[slot, 80 * (j - 1) : 80 * j, :]
                if j < 8:
                    y0 = y0 + cf(g, k, j) * w
                y1 = y1 + cf(g, k, 8 + j) * w
            y_scr[slot] = y0
            y1_scr[slot] = jnp.concatenate([y1.astype(BF16), jnp.zeros((48, 256), BF16)], 0)

        def finish(g, k, slot):
            z = jnp.dot(w8_scr[...], y1_scr[slot], preferred_element_type=F32)
            out = cf(g, k, 17) * (y_scr[slot] + z)
            for h in range(2):
                part = out[:, 128 * h : 128 * h + 128]
                for m, o in enumerate(VO):
                    vo2[pl.ds(g * 368 + (o * 8 + 2 * k + h), 8, stride=8), :] = part[8 * m : 8 * m + 8, :]
                for m, o in enumerate(SO):
                    so2[pl.ds(g * 240 + (o * 8 + 2 * k + h), 8, stride=8), :] = part[48 + 8 * m : 56 + 8 * m, :]

        ready(0)
        expand(0, 0, 0)
        y_scr[1] = jnp.zeros((80, 256), F32)
        y1_scr[1] = jnp.zeros((128, 256), BF16)

        @pl.loop(0, 8)
        def _(g):
            pl.when(g < 7)(lambda: ready(g + 1))
            for k in range(4):
                expand(jnp.minimum(g + 1, 7) if k == 3 else g, (k + 1) % 4, (k + 1) % 2)
                finish(jnp.maximum(g - 1, 0) if k == 0 else g, (k - 1) % 4, (k + 1) % 2)
                combine(g, k, k % 2)
            pl.when(g > 0)(lambda: emit(g - 1))

        finish(7, 3, 1)
        emit(7)
        for g in range(8):
            group(vo_hbm, vo, g, osems.at[0, g], True).wait()
            group(so_hbm, so, g, osems.at[1, g], True).wait()


def chem(early, vib, sp, rate, cnt, vr, kr, extra):
    hbm = pl.BlockSpec(memory_space=pl.ANY)
    n = len(extra)
    like = lambda v: jax.ShapeDtypeStruct(v.shape, v.dtype)
    outs = [like(vib), like(sp)] + ([like(v) for v in extra] if early else [])
    out = pl.pallas_call(
        functools.partial(chem_kernel, early),
        in_specs=[hbm] * (6 + n),
        out_specs=[hbm] * len(outs),
        out_shape=outs,
        input_output_aliases={6 + k: k + (2 if early else 0) for k in range(n)},
        scratch_shapes=[pltpu.VMEM((46, 46), F32), pltpu.VMEM((30, 30), F32), pltpu.SMEM((64,), jnp.int32),
                        pltpu.VMEM((64, 128), F32)]
        + [pltpu.VMEM((8, k, 8, 128), F32) for k in (46, 30, 46, 30)]
        + [pltpu.VMEM((48, 128), F32), pltpu.VMEM((32, 128), F32),
           pltpu.VMEM((640, 256), BF16), pltpu.VMEM((80, 128), BF16),
           pltpu.VMEM((17, 64, 128), F32), pltpu.VMEM((2, 640, 256), F32),
           pltpu.VMEM((2, 80, 256), F32), pltpu.VMEM((2, 128, 256), BF16),
           pltpu.SemaphoreType.DMA((2, 8)), pltpu.SemaphoreType.DMA((2, 8)), pltpu.SemaphoreType.DMA((4,))],
        compiler_params=pltpu.CompilerParams(vmem_limit_bytes=62 * 2**20),
        cost_estimate=pl.CostEstimate(flops=10**9, bytes_accessed=6 * 10**6, transcendentals=0),
        name="chemistry_early" if early else "chemistry_late",
    )(vr, kr, cnt, rate, vib, sp, *extra)
    return out[:2], out[2:]


def cell_flux(q, d):
    inv = 1.0 / q[0]
    u = q[d] * inv
    p = 0.4 * (q[4] - 0.5 * (q[1] * q[1] + q[2] * q[2] + q[3] * q[3]) * inv)
    f = [q[d], q[1] * u, q[2] * u, q[3] * u, (q[4] + p) * u]
    f[d] = f[d] + p
    return f, jnp.abs(u) + jnp.sqrt(1.4 * p * inv)


def recip(v):
    return pl.reciprocal(v, approx=True)


def side(v2, d0, d1, d2, d3):
    c0, c1, c2 = d1 - d0, d2 - d1, d3 - d2
    t1 = 3.0 * d1
    e0 = t1 - d0
    e1 = d1 + d2
    e2 = d3 - 3.0 * d2
    k = 13.0 / 3.0
    s0 = 1.6e-5 + (k * (c0 * c0) + e0 * e0)
    s1 = 1.6e-5 + (k * (c1 * c1) + e1 * e1)
    s2 = 1.6e-5 + (k * (c2 * c2) + e2 * e2)
    r0, r1, r2 = recip(s0), recip(s1), recip(s2)
    a0 = r0 * r0
    a1 = 6.0 * (r1 * r1)
    a2 = 3.0 * (r2 * r2)
    num = a0 * ((c0 + c0) + t1) + a1 * (e1 + d2) + a2 * (d2 - e2)
    den = a0 + a1 + a2
    return v2 + num * recip(6.0 * den)


def face(f, q, alpha):
    fd = [f[k + 1] - f[k] for k in range(5)]
    qd = [alpha * (q[k + 1] - q[k]) for k in range(5)]
    plus = side(f[2] + alpha * q[2], *[fd[k] + qd[k] for k in range(4)])
    m = [qd[k] - fd[k] for k in range(5)]
    minus = side(f[3] - alpha * q[3], m[4], m[3], m[2], m[1])
    return plus + minus


def weno_kernel(flow_ref, e_ref, xb_ref, yb_ref, xa_ref, ya_ref, own_ref, out_ref, xq, xf, xs, xg):
    even_x = lax.axis_index("gx") % 2 == 0
    even_y = lax.axis_index("gy") % 2 == 0
    xa, xb, ya, yb = xa_ref[...], xb_ref[...], ya_ref[0:8, :], yb_ref[0:8, :]
    up, dn = jnp.where(even_x, xb, xa), jnp.where(even_x, xa, xb)
    lq, rq = jnp.where(even_y, yb, ya), jnp.where(even_y, ya, yb)
    for c in range(5):
        xq[c, 5:8, :] = up[3 * c : 3 * c + 3, :]
        xq[c, 8:72, :] = e_ref[...] if c == 4 else flow_ref[c]
        xq[c, 72:75, :] = dn[3 * c : 3 * c + 3, :]
    one = jnp.ones((5, 128), F32)
    for c in range(5):
        fill = one if c in (0, 4) else 0.0 * one
        xq[c, 0:5, :] = fill
        xq[c, 75:80, :] = fill
    for g in range(10):
        sl = slice(8 * g, 8 * g + 8)
        f, s = cell_flux([xq[c, sl, :] for c in range(5)], 1)
        for c in range(5):
            xf[c, sl, :] = f[c]
        xs[sl, :] = s
    for g in range(9):
        b = 8 * g + 5
        n = 8 if g < 8 else 1
        alpha = xs[b : b + n, :]
        for o in range(1, 6):
            alpha = jnp.maximum(alpha, xs[b + o : b + o + n, :])
        for c in range(5):
            xg[c, 8 * g : 8 * g + n, :] = face(
                [xf[c, b + o : b + o + n, :] for o in range(6)],
                [xq[c, b + o : b + o + n, :] for o in range(6)],
                alpha,
            )

    lane = lax.broadcasted_iota(jnp.int32, (8, 128), 1)
    slot = lane % 16

    def shift(v, k):
        return v if k % 128 == 0 else pltpu.roll(v, (-k) % 128, 1)

    def strip(v):
        q = [shift(v, 3 * c) for c in range(5)]
        f, s = cell_flux(q, 2)
        ff = f[0]
        ss = s
        for c in range(1, 5):
            here = slot >= 3 * c
            ff = jnp.where(here, shift(f[c], -3 * c), ff)
            ss = jnp.where(here, shift(s, -3 * c), ss)
        return v, ff, ss

    lq, lfx, ls = strip(lq)
    oq, ofx, os_ = strip(own_ref[...])
    alpha = ls
    for v in (shift(ls, 1), shift(ls, 2), os_, shift(os_, 1), shift(os_, 2)):
        alpha = jnp.maximum(alpha, v)
    first = face(
        [lfx, shift(lfx, 1), shift(lfx, 2), ofx, shift(ofx, 1), shift(ofx, 2)],
        [lq, shift(lq, 1), shift(lq, 2), oq, shift(oq, 1), shift(oq, 2)],
        alpha,
    )
    for g in range(8):
        sl = slice(8 * g + 8, 8 * g + 16)
        q = [xq[c, sl, :] for c in range(5)]
        h = [
            jnp.where(lane < 64, shift(rq, 16 * g + 3 * c), shift(lq, 16 * g + 3 * c - 125)) for c in range(5)
        ]
        f, s = cell_flux(q, 2)
        hf, hs = cell_flux(h, 2)

        def six(a, b):
            out = []
            for o in range(-2, 4):
                if o == 0:
                    out.append(a)
                elif o > 0:
                    out.append(shift(jnp.where(lane < o, b, a), o))
                else:
                    out.append(shift(jnp.where(lane >= 128 + o, b, a), o))
            return out

        alphas = six(s, hs)
        alpha = alphas[0]
        for v in alphas[1:]:
            alpha = jnp.maximum(alpha, v)
        qs = [six(q[c], h[c]) for c in range(5)]
        for c in range(5):
            after = face(qs[2] if c == 0 else six(f[c], hf[c]), qs[c], alpha)
            before = jnp.where(lane == 0, shift(first, 16 * g + 3 * c), shift(after, -1))
            gx = xg[c, 8 * g + 1 : 8 * g + 9, :] - xg[c, 8 * g : 8 * g + 8, :]
            out_ref[c, 8 * g : 8 * g + 8, :] = q[c] - 0.05 * (gx + (after - before))


def weno(flow, e, xb, yb, xa, ya, own):
    vm = pl.BlockSpec(memory_space=pltpu.VMEM)
    return pl.pallas_call(
        weno_kernel,
        in_specs=[vm] * 7,
        out_specs=vm,
        out_shape=jax.ShapeDtypeStruct((5, 64, 128), F32),
        scratch_shapes=[pltpu.VMEM((5, 80, 128), F32), pltpu.VMEM((5, 80, 128), F32), pltpu.VMEM((80, 128), F32),
                        pltpu.VMEM((5, 72, 128), F32)],
        compiler_params=pltpu.CompilerParams(vmem_limit_bytes=20 * 2**20),
        cost_estimate=pl.CostEstimate(flops=10**7, bytes_accessed=10**6, transcendentals=0),
        name="euler_weno",
    )(flow, e, xb, yb, xa, ya, own)


def swaps(size, start):
    pairs = [(i % size, (i + 1) % size) for i in range(start, size, 2)]
    return pairs + [(b, a) for a, b in pairs]


def swapped(value, axis, start):
    return lax.ppermute(value, axis, swaps(lax.axis_size(axis), start))


def local(flow, vib, species, field_rate, substeps, vib_rates, kin_rates, level_energy, formation_heat):
    counts = substeps.reshape(-1)
    e, xa, xb, ya, yb, own = heat(
        flow, vib, species, field_rate, counts, vib_rates, kin_rates, level_energy, formation_heat
    )
    first, (xa, xb, ya, yb) = chem(
        True, vib, species, field_rate, counts, vib_rates, kin_rates, (xa, xb, ya, yb)
    )
    xb = swapped(xb, "gx", 1)
    yb = swapped(yb, "gy", 1)
    xa = swapped(xa, "gx", 0)
    ya = swapped(ya, "gy", 0)
    (vib_final, species_final), _ = chem(False, vib, species, field_rate, counts, vib_rates, kin_rates, first)
    return (weno(flow, e, xb, yb, xa, ya, own), vib_final, species_final)


def solution(mesh):
    tiled = P(None, "gx", "gy")
    return jax.shard_map(
        local,
        mesh=mesh,
        in_specs=(tiled, tiled, tiled, P("gx", "gy"), P("gx", "gy"), P(), P(), P(), P()),
        out_specs=(tiled, tiled, tiled),
        check_vma=False,
    )
```

time: 54.4 us -> 46.8 us (0.86)
  the two profiles are of different devices: /device:TPU:16 before, /device:TPU:478 now
where the time goes in v2:
time: 46.8 us; the launch traced here: 46.5 us
  starting transfers between devices  25.2 us (54%)
  Pallas kernels  20.5 us (44%)
  between operations  0.76 us (2%)
    ppermute x4, starting transfers between devices, swapped(): return lax.ppermute(value, axis, swaps(lax.axis_size(axis), start))  25.2 us
    pallas_call x2, Pallas kernels, chem(): pl.pallas_call(functools.partial(chem_kernel, early), in_specs=[hbm] * (6...  10.7 us
    pallas_call x1, Pallas kernels, heat(): pl.pallas_call(heat_kernel, in_specs=[hbm] * 9, out_specs=[vm] * 6, out_s...  5.57 us
    pallas_call x1, Pallas kernels, weno(): pl.pallas_call(weno_kernel, in_specs=[vm] * 7, out_specs=vm, out_shape=ja...  4.21 us
  transfers between devices with their start and end apart: 4, of which 0 were waited for; matrix products, arithmetic and copies ran while one was open for 0% of the time, Pallas kernels for 22%

profile of v2, /device:TPU:478, one launch (start us, length us, event | category | flops | bytes accessed | tf_op | source)
XLA Modules:
  0.0 46.5 jit_solution(10793088177445524856)
XLA Ops:
  0.6 5.6 %heat.1 = (f32[64,128]{1,0:T(8,128)}, f32[16,128]{1,0:T(8,128)}, f32[16,128]{1,0:T(8,128)}, f32[16,128]{1,0:T(8,128)}, f32[16,128]{1,0:T(8,128)}, /*index=5*/f32[8,128]{1,0:T(8,128)}) custom-call(f32[46,46]{1,0:T(8,128)} %vr_hbm.5, f32[30,30]{1,0:T(8,128)} %kr_hbm.5, f32[1,46]{1,0:T(1,128)} %bitcast.6, f32[1,30]{1,0:T(1,128)} %bitcast.7, s32[64]{0:T(128)} %bitcast.3, ...), custom_call_target="tpu_custom_call" | custom-call | flops 100000000 | bytes 3000000 | tf_op jit(solution)/shard_map/heat/pallas_call | solution.py:189
  6.2 0.3 chemistry_early.1
  6.6 2.2 %collective-permute-start = (f32[16,128]{1,0:T(8,128)}, f32[16,128]{1,0:T(8,128)S(1)}, u32[]{:S(2)}, u32[]{:S(2)}) collective-permute-start(f32[16,128]{1,0:T(8,128)} %get-tuple-element.22), channel_id=1, source_target_pairs={{32,64},{96,128},{160,192},{224,256},{288,320},{352,384},{416,448}... | collective-permute-start | bytes 24584 | tf_op jit(solution)/shard_map/ppermute | solution.py:511
  8.8 2.9 %collective-permute-start.1 = (f32[16,128]{1,0:T(8,128)}, f32[16,128]{1,0:T(8,128)S(1)}, u32[]{:S(2)}, u32[]{:S(2)}) collective-permute-start(f32[16,128]{1,0:T(8,128)} %get-tuple-element.23), channel_id=1, source_target_pairs={{1,2},{3,4},{5,6},{7,8},{9,10},{11,12},{13,14},{15,16},{17,18},{19... | collective-permute-start | bytes 24584 | tf_op jit(solution)/shard_map/ppermute | solution.py:511
  11.7 4.2 %collective-permute-start.2 = (f32[16,128]{1,0:T(8,128)}, f32[16,128]{1,0:T(8,128)S(1)}, u32[]{:S(2)}, u32[]{:S(2)}) collective-permute-start(f32[16,128]{1,0:T(8,128)} %get-tuple-element.24), channel_id=1, source_target_pairs={{0,32},{64,96},{128,160},{192,224},{256,288},{320,352},{384,416},{... | collective-permute-start | bytes 24584 | tf_op jit(solution)/shard_map/ppermute | solution.py:511
  15.9 15.9 %collective-permute-start.3 = (f32[16,128]{1,0:T(8,128)}, f32[16,128]{1,0:T(8,128)S(1)}, u32[]{:S(2)}, u32[]{:S(2)}) collective-permute-start(f32[16,128]{1,0:T(8,128)} %get-tuple-element.25), channel_id=1, source_target_pairs={{0,1},{2,3},{4,5},{6,7},{8,9},{10,11},{12,13},{14,15},{16,17},{18,... | collective-permute-start | bytes 24584 | tf_op jit(solution)/shard_map/ppermute | solution.py:511
  31.8 0.0 copy-start
  31.8 0.0 copy-start.1
  31.8 0.0 copy-start.2
  31.8 10.4 %chemistry_late.1 = (f32[46,64,128]{2,1,0:T(8,128)}, f32[30,64,128]{2,1,0:T(8,128)}) custom-call(f32[46,46]{1,0:T(8,128)} %vr_hbm.5, f32[30,30]{1,0:T(8,128)} %kr_hbm.5, s32[64]{0:T(128)} %bitcast.5, f32[64,128]{1,0:T(8,128)} %rate_hbm.5, f32[46,64,128]{2,1,0:T(8,128)} %vib_hbm.5, ...), custom_call_target="tpu_custom_call", output_to_operand_aliasing={{0}: (6, {}), {1}: (7, {})} | custom-call | flops 1000000000 | bytes 6000000 | tf_op jit(solution)/shard_map/chemistry_late/pallas_call | solution.py:335
  42.2 0.0 collective-permute-done.xb_ref
  42.2 0.0 collective-permute-done.1.yb_ref
  42.2 0.0 collective-permute-done.2.xa_ref
  42.2 0.0 collective-permute-done.3.ya_ref
  42.3 0.0 copy-done
  42.3 0.0 copy-done.1
  42.3 0.0 copy-done.2
  42.3 4.2 %euler_weno.1 = f32[5,64,128]{2,1,0:T(8,128)} custom-call(f32[5,64,128]{2,1,0:T(8,128)S(1)} %copy-done, f32[64,128]{1,0:T(8,128)S(1)} %copy-done.1, f32[16,128]{1,0:T(8,128)S(1)} %collective-permute-done.xb_ref, f32[16,128]{1,0:T(8,128)S(1)} %collective-permute-done.1.yb_ref, f32[16,128]{1,0:T(8,128)S(1)} %collective-permute-done.2.xa_ref, ...), custom_call_target="tpu_custom_call" | custom-call | flops 10000000 | bytes 1000000 | tf_op jit(solution)/shard_map/euler_weno/pallas_call | solution.py:492
Async XLA Ops:
  6.6 35.6 %collective-permute-start = (f32[16,128]{1,0:T(8,128)}, f32[16,128]{1,0:T(8,128)S(1)}, u32[]{:S(2)}, u32[]{:S(2)}) collective-permute-start(f32[16,128]{1,0:T(8,128)} %get-tuple-element.22), channel_id=1, source_target_pairs={{32,64},{96,128},{160,192},{224,256},{288,320},{352,384},{416,448}... | collective-permute-start | bytes 24584 | tf_op jit(solution)/shard_map/ppermute | solution.py:511
  8.8 33.5 %collective-permute-start.1 = (f32[16,128]{1,0:T(8,128)}, f32[16,128]{1,0:T(8,128)S(1)}, u32[]{:S(2)}, u32[]{:S(2)}) collective-permute-start(f32[16,128]{1,0:T(8,128)} %get-tuple-element.23), channel_id=1, source_target_pairs={{1,2},{3,4},{5,6},{7,8},{9,10},{11,12},{13,14},{15,16},{17,18},{19... | collective-permute-start | bytes 24584 | tf_op jit(solution)/shard_map/ppermute | solution.py:511
  11.7 30.6 %collective-permute-start.2 = (f32[16,128]{1,0:T(8,128)}, f32[16,128]{1,0:T(8,128)S(1)}, u32[]{:S(2)}, u32[]{:S(2)}) collective-permute-start(f32[16,128]{1,0:T(8,128)} %get-tuple-element.24), channel_id=1, source_target_pairs={{0,32},{64,96},{128,160},{192,224},{256,288},{320,352},{384,416},{... | collective-permute-start | bytes 24584 | tf_op jit(solution)/shard_map/ppermute | solution.py:511
  15.9 26.4 %collective-permute-start.3 = (f32[16,128]{1,0:T(8,128)}, f32[16,128]{1,0:T(8,128)S(1)}, u32[]{:S(2)}, u32[]{:S(2)}) collective-permute-start(f32[16,128]{1,0:T(8,128)} %get-tuple-element.25), channel_id=1, source_target_pairs={{0,1},{2,3},{4,5},{6,7},{8,9},{10,11},{12,13},{14,15},{16,17},{18,... | collective-permute-start | bytes 24584 | tf_op jit(solution)/shard_map/ppermute | solution.py:511
  31.8 10.5 %copy-start = (f32[5,64,128]{2,1,0:T(8,128)S(1)}, f32[5,64,128]{2,1,0:T(8,128)}, u32[]{:S(2)}) copy-start(f32[5,64,128]{2,1,0:T(8,128)} %flow_ref.1) | copy-start | bytes 491524
  31.8 10.5 %copy-start.1 = (f32[64,128]{1,0:T(8,128)S(1)}, f32[64,128]{1,0:T(8,128)}, u32[]{:S(2)}) copy-start(f32[64,128]{1,0:T(8,128)} %get-tuple-element.17.e_ref) | copy-start | bytes 98308
  31.8 10.5 %copy-start.2 = (f32[8,128]{1,0:T(8,128)S(1)}, f32[8,128]{1,0:T(8,128)}, u32[]{:S(2)}) copy-start(f32[8,128]{1,0:T(8,128)} %get-tuple-element.26.own_ref) | copy-start | bytes 12292

commit v3 on v2

--- a/solution.py
+++ b/solution.py
@@ -56,7 +56,10 @@
 
 
 def mm(a, b):
-    return jnp.dot(a, b, precision=HIGH, preferred_element_type=F32)
+    ah, bh = a.astype(BF16), b.astype(BF16)
+    al, bl = (a - ah.astype(F32)).astype(BF16), (b - bh.astype(F32)).astype(BF16)
+    out = jnp.dot(jnp.concatenate([ah, al], 1), jnp.concatenate([bh, bh], 0), preferred_element_type=F32)
+    return out + jnp.dot(ah, bl, preferred_element_type=F32)
 
 
 def load_pair(v2, s2, g, k):
@@ -164,7 +167,7 @@
         return out
 
     left = jnp.ones((8, 128), F32)
-    left, right = lax.fori_loop(0, 8, turn, (left, left))
+    left, right = lax.fori_loop(0, 8, turn, (left, left), unroll=4)
     left, right = sums(7, left, right)
     edge = {}
     for g in (0, 7):

time: 46.8 us -> 45.9 us (0.981)
  Pallas kernels: 20.5 us -> 19.9 us
where the time goes in v3:
time: 45.9 us; the launch traced here: 45.7 us
  starting transfers between devices  24.9 us (54%)
  Pallas kernels  19.9 us (43%)
  between operations  0.76 us (2%)
    ppermute x4, starting transfers between devices, swapped(): return lax.ppermute(value, axis, swaps(lax.axis_size(axis), start))  24.9 us
    pallas_call x2, Pallas kernels, chem(): pl.pallas_call(functools.partial(chem_kernel, early), in_specs=[hbm] * (6...  10.5 us
    pallas_call x1, Pallas kernels, heat(): pl.pallas_call(heat_kernel, in_specs=[hbm] * 9, out_specs=[vm] * 6, out_s...  5.26 us
    pallas_call x1, Pallas kernels, weno(): pl.pallas_call(weno_kernel, in_specs=[vm] * 7, out_specs=vm, out_shape=ja...  4.21 us
  transfers between devices with their start and end apart: 4, of which 0 were waited for; matrix products, arithmetic and copies ran while one was open for 0% of the time, Pallas kernels for 22%

profile of v3, /device:TPU:478, one launch (start us, length us, event | category | flops | bytes accessed | tf_op | source)
XLA Modules:
  0.0 45.7 jit_solution(13302025457455136692)
XLA Ops:
  0.6 5.3 %heat.1 = (f32[64,128]{1,0:T(8,128)}, f32[16,128]{1,0:T(8,128)}, f32[16,128]{1,0:T(8,128)}, f32[16,128]{1,0:T(8,128)}, f32[16,128]{1,0:T(8,128)}, /*index=5*/f32[8,128]{1,0:T(8,128)}) custom-call(f32[46,46]{1,0:T(8,128)} %vr_hbm.5, f32[30,30]{1,0:T(8,128)} %kr_hbm.5, f32[1,46]{1,0:T(1,128)} %bitcast.6, f32[1,30]{1,0:T(1,128)} %bitcast.7, s32[64]{0:T(128)} %bitcast.3, ...), custom_call_target="tpu_custom_call" | custom-call | flops 100000000 | bytes 3000000 | tf_op jit(solution)/shard_map/heat/pallas_call | solution.py:192
  5.9 0.3 chemistry_early.1
  6.3 2.2 %collective-permute-start = (f32[16,128]{1,0:T(8,128)}, f32[16,128]{1,0:T(8,128)S(1)}, u32[]{:S(2)}, u32[]{:S(2)}) collective-permute-start(f32[16,128]{1,0:T(8,128)} %get-tuple-element.22), channel_id=1, source_target_pairs={{32,64},{96,128},{160,192},{224,256},{288,320},{352,384},{416,448}... | collective-permute-start | bytes 24584 | tf_op jit(solution)/shard_map/ppermute | solution.py:514
  8.4 2.9 %collective-permute-start.1 = (f32[16,128]{1,0:T(8,128)}, f32[16,128]{1,0:T(8,128)S(1)}, u32[]{:S(2)}, u32[]{:S(2)}) collective-permute-start(f32[16,128]{1,0:T(8,128)} %get-tuple-element.23), channel_id=1, source_target_pairs={{1,2},{3,4},{5,6},{7,8},{9,10},{11,12},{13,14},{15,16},{17,18},{19... | collective-permute-start | bytes 24584 | tf_op jit(solution)/shard_map/ppermute | solution.py:514
  11.4 4.2 %collective-permute-start.2 = (f32[16,128]{1,0:T(8,128)}, f32[16,128]{1,0:T(8,128)S(1)}, u32[]{:S(2)}, u32[]{:S(2)}) collective-permute-start(f32[16,128]{1,0:T(8,128)} %get-tuple-element.24), channel_id=1, source_target_pairs={{0,32},{64,96},{128,160},{192,224},{256,288},{320,352},{384,416},{... | collective-permute-start | bytes 24584 | tf_op jit(solution)/shard_map/ppermute | solution.py:514
  15.6 15.6 %collective-permute-start.3 = (f32[16,128]{1,0:T(8,128)}, f32[16,128]{1,0:T(8,128)S(1)}, u32[]{:S(2)}, u32[]{:S(2)}) collective-permute-start(f32[16,128]{1,0:T(8,128)} %get-tuple-element.25), channel_id=1, source_target_pairs={{0,1},{2,3},{4,5},{6,7},{8,9},{10,11},{12,13},{14,15},{16,17},{18,... | collective-permute-start | bytes 24584 | tf_op jit(solution)/shard_map/ppermute | solution.py:514
  31.2 0.0 copy-start
  31.2 0.0 copy-start.1
  31.3 0.0 copy-start.2
  31.3 10.1 %chemistry_late.1 = (f32[46,64,128]{2,1,0:T(8,128)}, f32[30,64,128]{2,1,0:T(8,128)}) custom-call(f32[46,46]{1,0:T(8,128)} %vr_hbm.5, f32[30,30]{1,0:T(8,128)} %kr_hbm.5, s32[64]{0:T(128)} %bitcast.5, f32[64,128]{1,0:T(8,128)} %rate_hbm.5, f32[46,64,128]{2,1,0:T(8,128)} %vib_hbm.5, ...), custom_call_target="tpu_custom_call", output_to_operand_aliasing={{0}: (6, {}), {1}: (7, {})} | custom-call | flops 1000000000 | bytes 6000000 | tf_op jit(solution)/shard_map/chemistry_late/pallas_call | solution.py:338
  41.4 0.0 collective-permute-done.xb_ref
  41.4 0.0 collective-permute-done.1.yb_ref
  41.4 0.0 collective-permute-done.2.xa_ref
  41.4 0.0 collective-permute-done.3.ya_ref
  41.4 0.0 copy-done
  41.4 0.0 copy-done.1
  41.5 0.0 copy-done.2
  41.5 4.2 %euler_weno.1 = f32[5,64,128]{2,1,0:T(8,128)} custom-call(f32[5,64,128]{2,1,0:T(8,128)S(1)} %copy-done, f32[64,128]{1,0:T(8,128)S(1)} %copy-done.1, f32[16,128]{1,0:T(8,128)S(1)} %collective-permute-done.xb_ref, f32[16,128]{1,0:T(8,128)S(1)} %collective-permute-done.1.yb_ref, f32[16,128]{1,0:T(8,128)S(1)} %collective-permute-done.2.xa_ref, ...), custom_call_target="tpu_custom_call" | custom-call | flops 10000000 | bytes 1000000 | tf_op jit(solution)/shard_map/euler_weno/pallas_call | solution.py:495
Async XLA Ops:
  6.3 35.1 %collective-permute-start = (f32[16,128]{1,0:T(8,128)}, f32[16,128]{1,0:T(8,128)S(1)}, u32[]{:S(2)}, u32[]{:S(2)}) collective-permute-start(f32[16,128]{1,0:T(8,128)} %get-tuple-element.22), channel_id=1, source_target_pairs={{32,64},{96,128},{160,192},{224,256},{288,320},{352,384},{416,448}... | collective-permute-start | bytes 24584 | tf_op jit(solution)/shard_map/ppermute | solution.py:514
  8.4 33.0 %collective-permute-start.1 = (f32[16,128]{1,0:T(8,128)}, f32[16,128]{1,0:T(8,128)S(1)}, u32[]{:S(2)}, u32[]{:S(2)}) collective-permute-start(f32[16,128]{1,0:T(8,128)} %get-tuple-element.23), channel_id=1, source_target_pairs={{1,2},{3,4},{5,6},{7,8},{9,10},{11,12},{13,14},{15,16},{17,18},{19... | collective-permute-start | bytes 24584 | tf_op jit(solution)/shard_map/ppermute | solution.py:514
  11.4 30.1 %collective-permute-start.2 = (f32[16,128]{1,0:T(8,128)}, f32[16,128]{1,0:T(8,128)S(1)}, u32[]{:S(2)}, u32[]{:S(2)}) collective-permute-start(f32[16,128]{1,0:T(8,128)} %get-tuple-element.24), channel_id=1, source_target_pairs={{0,32},{64,96},{128,160},{192,224},{256,288},{320,352},{384,416},{... | collective-permute-start | bytes 24584 | tf_op jit(solution)/shard_map/ppermute | solution.py:514
  15.6 25.9 %collective-permute-start.3 = (f32[16,128]{1,0:T(8,128)}, f32[16,128]{1,0:T(8,128)S(1)}, u32[]{:S(2)}, u32[]{:S(2)}) collective-permute-start(f32[16,128]{1,0:T(8,128)} %get-tuple-element.25), channel_id=1, source_target_pairs={{0,1},{2,3},{4,5},{6,7},{8,9},{10,11},{12,13},{14,15},{16,17},{18,... | collective-permute-start | bytes 24584 | tf_op jit(solution)/shard_map/ppermute | solution.py:514
  31.2 10.2 %copy-start = (f32[5,64,128]{2,1,0:T(8,128)S(1)}, f32[5,64,128]{2,1,0:T(8,128)}, u32[]{:S(2)}) copy-start(f32[5,64,128]{2,1,0:T(8,128)} %flow_ref.1) | copy-start | bytes 491524
  31.2 10.2 %copy-start.1 = (f32[64,128]{1,0:T(8,128)S(1)}, f32[64,128]{1,0:T(8,128)}, u32[]{:S(2)}) copy-start(f32[64,128]{1,0:T(8,128)} %get-tuple-element.17.e_ref) | copy-start | bytes 98308
  31.3 10.2 %copy-start.2 = (f32[8,128]{1,0:T(8,128)S(1)}, f32[8,128]{1,0:T(8,128)}, u32[]{:S(2)}) copy-start(f32[8,128]{1,0:T(8,128)} %get-tuple-element.26.own_ref) | copy-start | bytes 12292

commit v4 on v3

--- a/solution.py
+++ b/solution.py
@@ -458,12 +458,12 @@
         [lq, shift(lq, 1), shift(lq, 2), oq, shift(oq, 1), shift(oq, 2)],
         alpha,
     )
+    before_it = shift(lq, 3)
+    both = [jnp.where((slot >= 3 * c) & (slot < 3 * c + 3), rq, before_it) for c in range(5)]
     for g in range(8):
         sl = slice(8 * g + 8, 8 * g + 16)
         q = [xq[c, sl, :] for c in range(5)]
-        h = [
-            jnp.where(lane < 64, shift(rq, 16 * g + 3 * c), shift(lq, 16 * g + 3 * c - 125)) for c in range(5)
-        ]
+        h = [shift(both[c], 16 * g + 3 * c) for c in range(5)]
         f, s = cell_flux(q, 2)
         hf, hs = cell_flux(h, 2)
 

time: 45.9 us -> 45.5 us (level)
  no operation moved by 1% of the time
where the time goes in v4:
time: 45.5 us; the launch traced here: 45.3 us
  starting transfers between devices  24.9 us (55%)
  Pallas kernels  19.5 us (43%)
  between operations  0.76 us (2%)
    ppermute x4, starting transfers between devices, swapped(): return lax.ppermute(value, axis, swaps(lax.axis_size(axis), start))  24.9 us
    pallas_call x2, Pallas kernels, chem(): pl.pallas_call(functools.partial(chem_kernel, early), in_specs=[hbm] * (6...  10.5 us
    pallas_call x1, Pallas kernels, heat(): pl.pallas_call(heat_kernel, in_specs=[hbm] * 9, out_specs=[vm] * 6, out_s...  5.26 us
    pallas_call x1, Pallas kernels, weno(): pl.pallas_call(weno_kernel, in_specs=[vm] * 7, out_specs=vm, out_shape=ja...  3.81 us
  transfers between devices with their start and end apart: 4, of which 0 were waited for; matrix products, arithmetic and copies ran while one was open for 0% of the time, Pallas kernels for 22%

profile of v4, /device:TPU:478, one launch (start us, length us, event | category | flops | bytes accessed | tf_op | source)
XLA Modules:
  0.0 45.3 jit_solution(9725479527818579369)
XLA Ops:
  0.6 5.3 %heat.1 = (f32[64,128]{1,0:T(8,128)}, f32[16,128]{1,0:T(8,128)}, f32[16,128]{1,0:T(8,128)}, f32[16,128]{1,0:T(8,128)}, f32[16,128]{1,0:T(8,128)}, /*index=5*/f32[8,128]{1,0:T(8,128)}) custom-call(f32[46,46]{1,0:T(8,128)} %vr_hbm.5, f32[30,30]{1,0:T(8,128)} %kr_hbm.5, f32[1,46]{1,0:T(1,128)} %bitcast.6, f32[1,30]{1,0:T(1,128)} %bitcast.7, s32[64]{0:T(128)} %bitcast.3, ...), custom_call_target="tpu_custom_call" | custom-call | flops 100000000 | bytes 3000000 | tf_op jit(solution)/shard_map/heat/pallas_call | solution.py:192
  5.9 0.3 chemistry_early.1
  6.3 2.2 %collective-permute-start = (f32[16,128]{1,0:T(8,128)}, f32[16,128]{1,0:T(8,128)S(1)}, u32[]{:S(2)}, u32[]{:S(2)}) collective-permute-start(f32[16,128]{1,0:T(8,128)} %get-tuple-element.22), channel_id=1, source_target_pairs={{32,64},{96,128},{160,192},{224,256},{288,320},{352,384},{416,448}... | collective-permute-start | bytes 24584 | tf_op jit(solution)/shard_map/ppermute | solution.py:514
  8.4 2.9 %collective-permute-start.1 = (f32[16,128]{1,0:T(8,128)}, f32[16,128]{1,0:T(8,128)S(1)}, u32[]{:S(2)}, u32[]{:S(2)}) collective-permute-start(f32[16,128]{1,0:T(8,128)} %get-tuple-element.23), channel_id=1, source_target_pairs={{1,2},{3,4},{5,6},{7,8},{9,10},{11,12},{13,14},{15,16},{17,18},{19... | collective-permute-start | bytes 24584 | tf_op jit(solution)/shard_map/ppermute | solution.py:514
  11.4 4.2 %collective-permute-start.2 = (f32[16,128]{1,0:T(8,128)}, f32[16,128]{1,0:T(8,128)S(1)}, u32[]{:S(2)}, u32[]{:S(2)}) collective-permute-start(f32[16,128]{1,0:T(8,128)} %get-tuple-element.24), channel_id=1, source_target_pairs={{0,32},{64,96},{128,160},{192,224},{256,288},{320,352},{384,416},{... | collective-permute-start | bytes 24584 | tf_op jit(solution)/shard_map/ppermute | solution.py:514
  15.6 15.6 %collective-permute-start.3 = (f32[16,128]{1,0:T(8,128)}, f32[16,128]{1,0:T(8,128)S(1)}, u32[]{:S(2)}, u32[]{:S(2)}) collective-permute-start(f32[16,128]{1,0:T(8,128)} %get-tuple-element.25), channel_id=1, source_target_pairs={{0,1},{2,3},{4,5},{6,7},{8,9},{10,11},{12,13},{14,15},{16,17},{18,... | collective-permute-start | bytes 24584 | tf_op jit(solution)/shard_map/ppermute | solution.py:514
  31.2 0.0 copy-start
  31.2 0.0 copy-start.1
  31.3 0.0 copy-start.2
  31.3 10.1 %chemistry_late.1 = (f32[46,64,128]{2,1,0:T(8,128)}, f32[30,64,128]{2,1,0:T(8,128)}) custom-call(f32[46,46]{1,0:T(8,128)} %vr_hbm.5, f32[30,30]{1,0:T(8,128)} %kr_hbm.5, s32[64]{0:T(128)} %bitcast.5, f32[64,128]{1,0:T(8,128)} %rate_hbm.5, f32[46,64,128]{2,1,0:T(8,128)} %vib_hbm.5, ...), custom_call_target="tpu_custom_call", output_to_operand_aliasing={{0}: (6, {}), {1}: (7, {})} | custom-call | flops 1000000000 | bytes 6000000 | tf_op jit(solution)/shard_map/chemistry_late/pallas_call | solution.py:338
  41.4 0.0 collective-permute-done.xb_ref
  41.4 0.0 collective-permute-done.1.yb_ref
  41.4 0.0 collective-permute-done.2.xa_ref
  41.4 0.0 collective-permute-done.3.ya_ref
  41.4 0.0 copy-done
  41.4 0.0 copy-done.1
  41.5 0.0 copy-done.2
  41.5 3.8 %euler_weno.1 = f32[5,64,128]{2,1,0:T(8,128)} custom-call(f32[5,64,128]{2,1,0:T(8,128)S(1)} %copy-done, f32[64,128]{1,0:T(8,128)S(1)} %copy-done.1, f32[16,128]{1,0:T(8,128)S(1)} %collective-permute-done.xb_ref, f32[16,128]{1,0:T(8,128)S(1)} %collective-permute-done.1.yb_ref, f32[16,128]{1,0:T(8,128)S(1)} %collective-permute-done.2.xa_ref, ...), custom_call_target="tpu_custom_call" | custom-call | flops 10000000 | bytes 1000000 | tf_op jit(solution)/shard_map/euler_weno/pallas_call | solution.py:495
Async XLA Ops:
  6.3 35.1 %collective-permute-start = (f32[16,128]{1,0:T(8,128)}, f32[16,128]{1,0:T(8,128)S(1)}, u32[]{:S(2)}, u32[]{:S(2)}) collective-permute-start(f32[16,128]{1,0:T(8,128)} %get-tuple-element.22), channel_id=1, source_target_pairs={{32,64},{96,128},{160,192},{224,256},{288,320},{352,384},{416,448}... | collective-permute-start | bytes 24584 | tf_op jit(solution)/shard_map/ppermute | solution.py:514
  8.4 33.0 %collective-permute-start.1 = (f32[16,128]{1,0:T(8,128)}, f32[16,128]{1,0:T(8,128)S(1)}, u32[]{:S(2)}, u32[]{:S(2)}) collective-permute-start(f32[16,128]{1,0:T(8,128)} %get-tuple-element.23), channel_id=1, source_target_pairs={{1,2},{3,4},{5,6},{7,8},{9,10},{11,12},{13,14},{15,16},{17,18},{19... | collective-permute-start | bytes 24584 | tf_op jit(solution)/shard_map/ppermute | solution.py:514
  11.4 30.1 %collective-permute-start.2 = (f32[16,128]{1,0:T(8,128)}, f32[16,128]{1,0:T(8,128)S(1)}, u32[]{:S(2)}, u32[]{:S(2)}) collective-permute-start(f32[16,128]{1,0:T(8,128)} %get-tuple-element.24), channel_id=1, source_target_pairs={{0,32},{64,96},{128,160},{192,224},{256,288},{320,352},{384,416},{... | collective-permute-start | bytes 24584 | tf_op jit(solution)/shard_map/ppermute | solution.py:514
  15.6 25.9 %collective-permute-start.3 = (f32[16,128]{1,0:T(8,128)}, f32[16,128]{1,0:T(8,128)S(1)}, u32[]{:S(2)}, u32[]{:S(2)}) collective-permute-start(f32[16,128]{1,0:T(8,128)} %get-tuple-element.25), channel_id=1, source_target_pairs={{0,1},{2,3},{4,5},{6,7},{8,9},{10,11},{12,13},{14,15},{16,17},{18,... | collective-permute-start | bytes 24584 | tf_op jit(solution)/shard_map/ppermute | solution.py:514
  31.2 10.2 %copy-start = (f32[5,64,128]{2,1,0:T(8,128)S(1)}, f32[5,64,128]{2,1,0:T(8,128)}, u32[]{:S(2)}) copy-start(f32[5,64,128]{2,1,0:T(8,128)} %flow_ref.1) | copy-start | bytes 491524
  31.2 10.2 %copy-start.1 = (f32[64,128]{1,0:T(8,128)S(1)}, f32[64,128]{1,0:T(8,128)}, u32[]{:S(2)}) copy-start(f32[64,128]{1,0:T(8,128)} %get-tuple-element.17.e_ref) | copy-start | bytes 98308
  31.3 10.2 %copy-start.2 = (f32[8,128]{1,0:T(8,128)S(1)}, f32[8,128]{1,0:T(8,128)}, u32[]{:S(2)}) copy-start(f32[8,128]{1,0:T(8,128)} %get-tuple-element.26.own_ref) | copy-start | bytes 12292
